TPU v7x, 128 devices: a whole 4x4x4 slice. The times are simulated.
128 devices in a mesh: seq: 32 (over x, z, y_lo), tp: 4 (over y_hi, core).
Axes of the slice: x: 4, y: 4 (y_hi: 2, y_lo: 2; y = y_hi * 2 + y_lo), z: 4, core: 2. Of those that a mesh axis runs over, the one named last changes fastest.
Arguments:
- context: bfloat16 [65536, 2048], P('seq'), may hold values from -40 to 40
- latent_in: bfloat16 [1024, 2048], P('seq'), may hold values from -24 to 24
- cutoff: int32 [1024], replicated, may hold values from 0 to 65535, as said below
- wq_cross: bfloat16 [2048, 2048], P(None, 'tp'), may hold values from -0.6 to 0.6
- wk_cross: bfloat16 [2048, 2048], P(None, 'tp'), may hold values from -0.6 to 0.6
- wv_cross: bfloat16 [2048, 2048], P(None, 'tp'), may hold values from -0.125 to 0.125
- wo_cross: bfloat16 [2048, 2048], P('tp'), may hold values from -0.125 to 0.125
- wq_self: bfloat16 [2048, 2048], P(None, 'tp'), may hold values from -0.6 to 0.6
- wk_self: bfloat16 [2048, 2048], P(None, 'tp'), may hold values from -0.6 to 0.6
- wv_self: bfloat16 [2048, 2048], P(None, 'tp'), may hold values from -0.125 to 0.125
- wo_self: bfloat16 [2048, 2048], P('tp'), may hold values from -0.125 to 0.125
Outputs:
- latent_out: bfloat16 [1024, 2048], P('seq')
Inputs may be any that keep to these rules, and one draw needn't show every extreme that they name: `cutoff`: strictly increasing; the last entry is 65535.
All inputs are finite; a program needn't handle non-finite values.
Results may differ from a plain program's by a relative error of at most 0.012.
Values may be sent and summed in bfloat16 or wider, within the bound.
No kernel may reach another device: no remote copies, remote signals or barrier semaphores. Data moves between devices by JAX's collectives and lax.ppermute only.
A program may use at most 192 MiB of HBM per device.

v0:
```python
import functools

import jax
import jax.numpy as jnp
import numpy as np
from jax import lax
from jax.experimental import pallas as pl
from jax.experimental.pallas import tpu as pltpu
from jax.sharding import Mesh, PartitionSpec as P

HEAD_DIM = 128
EPSILON = 1e-05
MASKED_SCORE = -1e30
LOG2E = 1.4426950408889634
MIB = 1 << 20
F32 = jnp.float32
BF16 = jnp.bfloat16

VMEM = pl.BlockSpec(memory_space=pltpu.VMEM)
SMEM = pl.BlockSpec(memory_space=pltpu.SMEM)


def shape_of(dims, dtype=BF16):
    return jax.ShapeDtypeStruct(dims, dtype)


def params(mib):
    return pltpu.CompilerParams(vmem_limit_bytes=mib * MIB)


def cost(flops, nbytes, trans=0):
    return pl.CostEstimate(flops=flops, bytes_accessed=nbytes, transcendentals=trans)


def dot(a, b):
    return jnp.dot(a, b, preferred_element_type=F32)


def dot_t(a, b):
    return lax.dot_general(a, b, (((1,), (1,)), ((), ())), preferred_element_type=F32)


def inv_rms(tile):
    return lax.rsqrt(jnp.mean(tile * tile, axis=-1, keepdims=True) + EPSILON)


def query_kernel(latent_ref, wq_ref, out_ref):
    tile = latent_ref[...].astype(F32)
    normed = (tile * inv_rms(tile)).astype(BF16)
    factor = HEAD_DIM ** (-0.5) * LOG2E
    out_ref[...] = (dot(normed, wq_ref[...]) * factor).astype(BF16)


def project_queries(latent_in, wq):
    rows, width = latent_in.shape
    cols = wq.shape[1]
    return pl.pallas_call(
        query_kernel,
        out_shape=shape_of((rows, cols)),
        in_specs=[VMEM, VMEM],
        out_specs=VMEM,
        compiler_params=params(8),
        cost_estimate=cost(2 * rows * width * cols, 2 * width * cols),
        name="queries",
    )(latent_in, wq)


def context_kernel(first, step, context_ref, w_ref, after_ref, out_ref):
    def rows_from(i, _):
        there = pl.ds(pl.multiple_of(first + i * step, step), step)
        tile = context_ref[there, :]
        product = dot(tile, w_ref[...]) * inv_rms(tile.astype(F32))
        out_ref[pl.ds(pl.multiple_of(i * step, step), step), :] = product.astype(BF16)
        return 0

    lax.fori_loop(0, out_ref.shape[0] // step, rows_from, 0, unroll=True)


def project_context(context, weight, after, name, first, rows):
    width = context.shape[1]
    cols = weight.shape[1]
    return pl.pallas_call(
        functools.partial(context_kernel, first, min(512, rows)),
        out_shape=shape_of((rows, cols)),
        in_specs=[VMEM, VMEM, pl.BlockSpec(memory_space=pl.ANY)],
        out_specs=VMEM,
        compiler_params=params(20),
        cost_estimate=cost(2 * rows * width * cols, 2 * (rows * width + width * cols)),
        name=name,
    )(context, weight, after)


def packed_totals(totals):
    lane = lax.broadcasted_iota(jnp.int32, totals[0].shape, 1)
    held = jnp.zeros(totals[0].shape, F32)
    for head, total in enumerate(totals):
        held = jnp.where(lane == head, total, held)
    high = held.astype(BF16).astype(F32)
    rest = held - high
    mid = rest.astype(BF16).astype(F32)
    low = rest - mid
    return (high + pltpu.roll(mid, 4, 1) + pltpu.roll(low, 8, 1)).astype(BF16)


def spread_matrix(heads):
    dims = (HEAD_DIM, heads * HEAD_DIM)
    row = lax.broadcasted_iota(jnp.int32, dims, 0)
    head = lax.broadcasted_iota(jnp.int32, dims, 1) >> 7
    return jnp.where((row < 12) & ((row & 3) == head), 1.0, 0.0).astype(BF16)


def cross_kernel(offsets, ids_ref, cutoff_ref, cut_ref, k_ref, more_ref, v_ref, *rest):
    blocks = len(offsets)
    q_refs, out_refs, bias = rest[:blocks], rest[blocks : 2 * blocks], rest[2 * blocks]
    rows, cols = q_refs[0].shape
    heads = cols // HEAD_DIM
    places = v_ref.shape[0]
    step = 512
    first_pos = ids_ref[2]
    starts = [((ids_ref[0] + offset) & 3) * rows for offset in offsets]
    lowest = functools.reduce(jnp.minimum, [cutoff_ref[start] for start in starts])
    highest = functools.reduce(jnp.maximum, [cutoff_ref[start + rows - 1] for start in starts])
    lowest, highest = lowest - first_pos, highest - first_pos
    spans = [slice(head * HEAD_DIM, (head + 1) * HEAD_DIM) for head in range(heads)]

    def stacked(pieces):
        return pieces[0] if blocks == 1 else jnp.concatenate(pieces, axis=0)

    def put(span, value):
        for i, out_ref in enumerate(out_refs):
            out_ref[:, span] = value[i * rows : (i + 1) * rows].astype(BF16)

    @pl.when(highest < 0)
    def _():
        put(slice(0, cols), jnp.zeros((blocks * rows, cols), BF16))
        put(
            slice(cols, cols + HEAD_DIM),
            packed_totals([jnp.full((blocks * rows, HEAD_DIM), MASKED_SCORE, F32)] * heads),
        )

    def attend(masked):
        ones = jnp.ones((step, HEAD_DIM), BF16)
        if masked:
            cut = stacked(
                [cut_ref[pl.ds(pl.multiple_of(start, rows), rows), :] for start in starts]
            )
            cut = cut - first_pos
            order = lax.broadcasted_iota(jnp.int32, cut.shape, 1)
            for place in range(0, places, HEAD_DIM):
                bias[:, place : place + HEAD_DIM] = jnp.where(
                    order + place <= cut, 0.0, MASKED_SCORE
                )

        def scores_of(head):
            queries = stacked([q_ref[:, spans[head]] for q_ref in q_refs])
            keys = jnp.concatenate([k_ref[:, spans[head]], more_ref[:, spans[head]]], axis=0)
            scores = dot_t(queries, keys)
            return scores + bias[...] if masked else scores

        totals = []
        scores = scores_of(0)
        for head in range(heads):
            peak = jnp.max(scores, axis=1, keepdims=True)
            later = scores_of(head + 1) if head + 1 < heads else None
            both = jnp.zeros((blocks * rows, 2 * HEAD_DIM), F32)
            for place in range(0, places, step):
                here = slice(place, place + step)
                probs = jnp.exp2(scores[:, here] - peak).astype(BF16)
                both += dot(probs, jnp.concatenate([v_ref[here, spans[head]], ones], axis=1))
            total = both[:, HEAD_DIM:]
            put(spans[head], both[:, :HEAD_DIM] / total)
            whole = jnp.log2(total) + peak
            totals.append(jnp.where(cut >= 0, whole, MASKED_SCORE) if masked else whole)
            scores = later
        put(slice(cols, cols + HEAD_DIM), packed_totals(totals))

    @pl.when(highest >= 0)
    def _():
        attend(True)


def cross_attend(offsets, ids, cutoff, queries, keys, values, cut_wide):
    blocks = len(offsets)
    rows, cols = queries[0].shape
    places = values.shape[0]
    return pl.pallas_call(
        functools.partial(cross_kernel, offsets),
        out_shape=[shape_of((rows, cols + HEAD_DIM))] * blocks,
        in_specs=[SMEM, SMEM] + [VMEM] * (4 + blocks),
        out_specs=[VMEM] * blocks,
        scratch_shapes=[pltpu.VMEM((blocks * rows, places), F32)],
        compiler_params=params(20 if blocks == 1 else 32),
        cost_estimate=cost(
            blocks * 8 * rows * places * cols, 4 * places * cols, blocks * rows * places * 4
        ),
        name="cross",
    )(ids, cutoff, cut_wide, *keys, values, *queries)


def blend(parts, spread, heads):
    cols = heads * HEAD_DIM
    totals = [dot(part[:, cols:], spread) for part in parts]
    peak = functools.reduce(jnp.maximum, totals)
    weights = [jnp.exp2(total - peak) for total in totals]
    weight_sum = functools.reduce(jnp.add, weights)
    mixed = functools.reduce(
        jnp.add, [w * part[:, :cols].astype(F32) for w, part in zip(weights, parts)]
    )
    return mixed / weight_sum, peak + jnp.log2(weight_sum)


def blend_kernel(a_ref, b_ref, c_ref, d_ref, out_ref):
    rows, width = a_ref.shape
    heads = width // HEAD_DIM - 1
    cols = heads * HEAD_DIM
    mixed, whole = blend(
        [a_ref[...], b_ref[...], c_ref[...], d_ref[...]], spread_matrix(heads), heads
    )
    out_ref[:, :cols] = mixed.astype(BF16)
    out_ref[:, cols:] = packed_totals(
        [whole[:, head * HEAD_DIM : (head + 1) * HEAD_DIM] for head in range(heads)]
    )


def blend_parts(parts):
    return pl.pallas_call(
        blend_kernel,
        out_shape=shape_of(parts[0].shape),
        in_specs=[VMEM] * 4,
        out_specs=VMEM,
        compiler_params=params(16),
        name="blend",
    )(*parts)


def cross_output_kernel(parts_ref, wo_ref, out_ref):
    heads = parts_ref.shape[2] // HEAD_DIM - 1
    parts = [parts_ref[i] for i in range(parts_ref.shape[0])]
    mixed, _ = blend(parts, spread_matrix(heads), heads)
    out_ref[...] = dot(mixed.astype(BF16), wo_ref[...]).astype(BF16)


def cross_output(parts, wo):
    return pl.pallas_call(
        cross_output_kernel,
        out_shape=shape_of((parts.shape[1], wo.shape[1])),
        in_specs=[VMEM] * 2,
        out_specs=VMEM,
        compiler_params=params(16),
        name="cross_output",
    )(parts, wo)


def self_project_kernel(
    ids_ref, latent_ref, one_ref, two_ref, wq_ref, wk_ref, wv_ref, state_ref, *rest
):
    outs, held = rest[:4], rest[4]
    rows, cols = held.shape[1:]
    state = latent_ref[...].astype(F32) + (one_ref[...].astype(F32) + two_ref[...].astype(F32))
    state_ref[...] = state
    normed = (state * inv_rms(state)).astype(BF16)
    held[0] = (dot(normed, wq_ref[...]) * (HEAD_DIM ** (-0.5) * LOG2E)).astype(BF16)
    held[1] = dot(normed, wk_ref[...]).astype(BF16)
    held[2] = dot(normed, wv_ref[...]).astype(BF16)
    for offset in range(4):
        head = lax.rem(ids_ref[0] + offset, 4)
        span = pl.ds(pl.multiple_of(head * HEAD_DIM, HEAD_DIM), HEAD_DIM)
        for part in range(3):
            outs[offset][:, part * HEAD_DIM : (part + 1) * HEAD_DIM] = held[part, :, span]


def self_project(ids, latent_in, one, two, wq, wk, wv):
    rows, width = latent_in.shape
    return pl.pallas_call(
        self_project_kernel,
        out_shape=[shape_of((rows, width), F32)] + [shape_of((rows, 3 * HEAD_DIM))] * 4,
        in_specs=[SMEM] + [VMEM] * 6,
        out_specs=[VMEM] * 5,
        scratch_shapes=[pltpu.VMEM((3, rows, wq.shape[1]), BF16)],
        compiler_params=params(24),
        name="self_project",
    )(ids, latent_in, one, two, wq, wk, wv)


def self_kernel(ids_ref, a_ref, b_ref, c_ref, d_ref, kv_ref, *outs):
    rows = a_ref.shape[0]
    groups, group_rows, _ = kv_ref.shape
    own_a, own_b, stride_a, stride_b, own_y = (ids_ref[i] for i in (0, 1, 3, 4, 5))
    q = jnp.concatenate([ref[:, :HEAD_DIM] for ref in (a_ref, b_ref, c_ref, d_ref)], axis=0)
    k = jnp.concatenate([kv_ref[i, :, :HEAD_DIM] for i in range(groups)], axis=0)
    v = jnp.concatenate([kv_ref[i, :, HEAD_DIM:] for i in range(groups)], axis=0)
    scores = dot_t(q, k)
    q_row = lax.broadcasted_iota(jnp.int32, scores.shape, 0)
    k_row = lax.broadcasted_iota(jnp.int32, scores.shape, 1)
    shift = rows.bit_length() - 1
    q_a = (own_a - (q_row >> shift)) & 3
    q_place = q_a * stride_a + (q_row & (rows - 1)) + (own_b * stride_b + own_y * rows)
    group = k_row >> (group_rows.bit_length() - 1)
    k_a = (own_a - (k_row >> shift)) & 3
    k_place = k_a * stride_a + (group >> 1) * stride_b + (group & 1) * rows + (k_row & (rows - 1))
    scores = jnp.where(k_place <= q_place, scores, MASKED_SCORE)
    peak = jnp.max(scores, axis=1, keepdims=True)
    probs = jnp.exp2(scores - peak).astype(BF16)
    both = dot(probs, jnp.concatenate([v, jnp.ones(v.shape, BF16)], axis=1))
    result = (both[:, :HEAD_DIM] / both[:, HEAD_DIM:]).astype(BF16)
    for offset in range(4):
        outs[offset][...] = result[offset * rows : (offset + 1) * rows]


def self_attend(ids, parts, kv):
    rows = parts[0].shape[0]
    return pl.pallas_call(
        self_kernel,
        out_shape=[shape_of((rows, HEAD_DIM))] * 4,
        in_specs=[SMEM] + [VMEM] * 5,
        out_specs=[VMEM] * 4,
        compiler_params=params(16),
        name="self_attend",
    )(ids, *parts, kv)


def self_output_kernel(ids_ref, a_ref, b_ref, c_ref, d_ref, wo_ref, out_ref, held):
    for offset, ref in enumerate((a_ref, b_ref, c_ref, d_ref)):
        head = lax.rem(ids_ref[0] + offset, 4)
        held[:, pl.ds(pl.multiple_of(head * HEAD_DIM, HEAD_DIM), HEAD_DIM)] = ref[...]
    out_ref[...] = dot(held[...], wo_ref[...]).astype(BF16)


def self_output(ids, parts, wo):
    rows = parts[0].shape[0]
    return pl.pallas_call(
        self_output_kernel,
        out_shape=shape_of((rows, wo.shape[1])),
        in_specs=[SMEM] + [VMEM] * 5,
        out_specs=VMEM,
        scratch_shapes=[pltpu.VMEM((rows, wo.shape[0]), BF16)],
        compiler_params=params(16),
        name="self_output",
    )(ids, *parts, wo)


def moved(tensor, axis, size, offset):
    return lax.ppermute(tensor, axis, [(i, (i + offset) % size) for i in range(size)])


PLANE = ("x", "z", "core")
WHOLE = ("x", "z", "y_lo", "y_hi", "core")


def turned(tensor, axis, offset):
    pairs = []
    for x in range(4):
        for z in range(4):
            for core in range(2):
                if (axis == "a") == (core == 0):
                    to = ((x + offset) % 4, z)
                else:
                    to = (x, (z + offset) % 4)
                pairs.append(((x * 4 + z) * 2 + core, (to[0] * 4 + to[1]) * 2 + core))
    return lax.ppermute(tensor, PLANE, pairs)


def exchanged(tensor):
    order = np.arange(128).reshape(4, 4, 2, 2, 2)
    groups = []
    for y_hi in range(2):
        for a in range(4):
            groups.append(order[a, :, :, y_hi, 0].reshape(-1).tolist())
            groups.append(order[:, a, :, y_hi, 1].reshape(-1).tolist())
    return lax.all_to_all(tensor, WHOLE, 0, 0, axis_index_groups=groups)


def summed_over_tp(part):
    other = moved(part, "core", 2, 1)
    pair = (part.astype(F32) + other.astype(F32)).astype(BF16)
    return pair, moved(pair, "y_hi", 2, 1)


def on_device(
    context,
    latent_in,
    cutoff,
    wq_cross,
    wk_cross,
    wv_cross,
    wo_cross,
    wq_self,
    wk_self,
    wv_self,
    wo_self,
):
    x, z, y_lo = lax.axis_index("x"), lax.axis_index("z"), lax.axis_index("y_lo")
    first_core = lax.axis_index("core") == 0
    a = jnp.where(first_core, x, z)
    b = jnp.where(first_core, z, x)
    rows = latent_in.shape[0]
    stride_a = jnp.where(first_core, 8 * rows, 2 * rows)
    stride_b = jnp.where(first_core, 2 * rows, 8 * rows)
    first_pos = ((x * 4 + z) * 2 + y_lo) * context.shape[0]
    ids = jnp.stack([a, b, first_pos, stride_a, stride_b, y_lo]).astype(jnp.int32)
    turned_cutoff = cutoff.reshape(4, 4, 2 * rows).transpose(1, 0, 2).reshape(-1)
    cutoff = jnp.where(first_core, cutoff, turned_cutoff)
    cut_wide = jnp.broadcast_to(cutoff[:, None], (cutoff.shape[0], HEAD_DIM))

    own = project_queries(latent_in, wq_cross)
    other = moved(own, "y_lo", 2, 1)
    pair = jnp.where(
        y_lo == 0, jnp.concatenate([own, other]), jnp.concatenate([other, own])
    )
    half = context.shape[0] // 2
    keys = [project_context(context, wk_cross, pair, "keys", 0, half)]
    came = {offset: turned(pair, "b", offset) for offset in (2, 1, 3)}
    ring = [pair] + [came[offset] for offset in (1, 2, 3)]
    pieces = [
        lax.dynamic_index_in_dim(jnp.stack(ring), (b - place) & 3, 0, False) for place in range(4)
    ]
    mine = jnp.concatenate(pieces)
    keys.append(project_context(context, wk_cross, mine, "keys", half, half))
    values = project_context(context, wv_cross, mine, "values", 0, 2 * half)
    blocks = {0: mine}
    for offset in (2, 3, 1):
        blocks[(4 - offset) % 4] = turned(mine, "a", offset)

    parts = []
    for offsets in ((2, 1), (3,), (0,)):
        queries = [blocks[offset] for offset in offsets]
        made = cross_attend(offsets, ids, cutoff, queries, keys, values, cut_wide)
        for offset, part in zip(offsets, made):
            parts.append(turned(part, "a", offset) if offset else part)
    mixed = blend_parts(parts)
    mixed = mixed.reshape(8, rows, mixed.shape[1])
    mixed = exchanged(mixed)
    cross_part = cross_output(mixed, wo_cross)
    one, two = summed_over_tp(cross_part)

    state, *sent = self_project(ids, latent_in, one, two, wq_self, wk_self, wv_self)
    came = {o: turned(sent[o], "a", o) for o in (2, 1, 3)}
    parts = [sent[0]] + [came[o] for o in (1, 2, 3)]
    kv = jnp.concatenate([part[:, HEAD_DIM:] for part in parts])
    kv = exchanged(jnp.broadcast_to(kv[None], (8,) + kv.shape))
    outs = self_attend(ids, parts, kv)
    came = {o: turned(outs[o], "a", -o) for o in (2, 1, 3)}
    outs = [outs[0]] + [came[o] for o in (1, 2, 3)]
    self_part = self_output(ids, outs, wo_self)
    one, two = summed_over_tp(self_part)
    return (state + (one.astype(F32) + two.astype(F32))).astype(BF16)


def solution(mesh):
    fine = Mesh(
        mesh.devices.reshape(4, 4, 2, 2, 2), ("x", "z", "y_lo", "y_hi", "core")
    )
    seq, tp = ("x", "z", "y_lo"), ("y_hi", "core")
    in_specs = (
        P(seq, None),
        P(seq, None),
        P(),
        P(None, tp),
        P(None, tp),
        P(None, tp),
        P(tp, None),
        P(None, tp),
        P(None, tp),
        P(None, tp),
        P(tp, None),
    )
    return jax.shard_map(
        on_device, mesh=fine, in_specs=in_specs, out_specs=P(seq, None), check_vma=False
    )
```

profile of v0, /device:TPU:1, one launch (start us, length us, event | category | flops | bytes accessed | tf_op | source)
XLA Modules:
  0.0 111.4 jit_solution(17195142325096722922)
XLA Ops:
  0.0 1.7 %copy-done.4 = bf16[2048,512]{1,0:T(8,128)(2,1)S(1)} copy-done((bf16[2048,512]{1,0:T(8,128)(2,1)S(1)}, bf16[2048,512]{1,0:T(8,128)(2,1)}, u32[]{:S(2)}) %copy-start.4) | copy-done | bytes 2097176
  1.7 0.9 copy-done.8
  2.7 0.5 queries.1
  3.2 2.2 %collective-permute-start = (bf16[32,512]{1,0:T(8,128)(2,1)S(1)}, bf16[32,512]{1,0:T(8,128)(2,1)S(1)}, u32[]{:S(2)}, u32[]{:S(2)}) collective-permute-start(bf16[32,512]{1,0:T(8,128)(2,1)S(1)} %queries.1), channel_id=1, source_target_pairs={{0,4},{4,0},{1,5},{5,1},{2,6},{6,2},{3,7},{7,3},{8,12},{12,8},{9,1... | collective-permute-start | bytes 98312 | tf_op jit(solution)/shard_map/ppermute | solution.py:343
  5.6 1.0 collective-permute-done
  6.7 2.7 %collective-permute-start.3 = (bf16[64,512]{1,0:T(8,128)(2,1)S(1)}, bf16[64,512]{1,0:T(8,128)(2,1)S(1)}, u32[]{:S(2)}, u32[]{:S(2)}) collective-permute-start(bf16[64,512]{1,0:T(8,128)(2,1)S(1)} %maximum_select_fusion.after_ref), channel_id=1, source_target_pairs={{0,24},{1,97},{8,0},{9,105},{16,8},{17,113},{24,16},{25,121},{32,5... | collective-permute-start | bytes 196616 | tf_op jit(solution)/shard_map/ppermute | solution.py:360
  9.4 0.5 collective-permute-start.2
  9.9 0.6 collective-permute-start.1
  10.6 3.4 %copy-done = bf16[2048,2048]{1,0:T(8,128)(2,1)S(1)} copy-done((bf16[2048,2048]{1,0:T(8,128)(2,1)S(1)}, bf16[2048,2048]{1,0:T(8,128)(2,1)}, u32[]{:S(2)}) %copy-start) | copy-done | bytes 8388632
  13.9 2.3 %keys.2.k_ref = bf16[1024,512]{1,0:T(8,128)(2,1)S(1)} custom-call(bf16[2048,2048]{1,0:T(8,128)(2,1)S(1)} %copy-done, bf16[2048,512]{1,0:T(8,128)(2,1)S(1)} %copy-done.1, bf16[64,512]{1,0:T(8,128)(2,1)S(1)} %maximum_select_fusion.after_ref), custom_call_target="tpu_custom_call" | custom-call | flops 2147483648 | bytes 6291456 | tf_op jit(solution)/shard_map/keys/pallas_call | solution.py:82
  16.4 3.7 %collective-permute-start.4 = (bf16[256,512]{1,0:T(8,128)(2,1)S(1)}, bf16[256,512]{1,0:T(8,128)(2,1)S(1)}, u32[]{:S(2)}, u32[]{:S(2)}) collective-permute-start(bf16[256,512]{1,0:T(8,128)(2,1)S(1)} %pad_maximum_fusion.1.after_ref.rest_0_), channel_id=1, source_target_pairs={{0,64},{1,17},{8,72},{9,25},{16,80},{17,1},{24,88},{25,9},{32,96},... | collective-permute-start | bytes 786440 | tf_op jit(solution)/shard_map/ppermute | solution.py:360
  20.1 0.4 collective-permute-start.5
  20.6 1.0 collective-permute-start.8
  21.6 4.5 %values.1.v_ref = bf16[2048,512]{1,0:T(8,128)(2,1)S(1)} custom-call(bf16[2048,2048]{1,0:T(8,128)(2,1)S(1)} %copy-done, bf16[2048,512]{1,0:T(8,128)(2,1)S(1)} %copy-done.10, bf16[256,512]{1,0:T(8,128)(2,1)S(1)} %pad_maximum_fusion.1.after_ref.rest_0_), custom_call_target="tpu_custom_call" | custom-call | flops 4294967296 | bytes 10485760 | tf_op jit(solution)/shard_map/values/pallas_call | solution.py:82
  26.1 2.3 %keys.3.more_ref = bf16[1024,512]{1,0:T(8,128)(2,1)S(1)} custom-call(bf16[2048,2048]{1,0:T(8,128)(2,1)S(1)} %copy-done, bf16[2048,512]{1,0:T(8,128)(2,1)S(1)} %copy-done.1, bf16[256,512]{1,0:T(8,128)(2,1)S(1)} %pad_maximum_fusion.1.after_ref.rest_0_), custom_call_target="tpu_custom_call" | custom-call | flops 2147483648 | bytes 6291456 | tf_op jit(solution)/shard_map/keys/pallas_call | solution.py:82
  28.7 6.8 %cross.3 = (bf16[256,640]{1,0:T(8,128)(2,1)S(1)}, bf16[256,640]{1,0:T(8,128)(2,1)S(1)}) custom-call(s32[6]{0:T(128)S(1)} %stack.55.ids_ref, s32[1024]{0:T(1024)S(1)} %broadcast_select_fusion.cutoff_ref, s32[1024,128]{1,0:T(8,128)S(1)} %broadcast_in_dim.4.cut_ref, bf16[1024,512]{1,0:T(8,128)(2,1)S(1)} %keys.2.k_ref, bf16[1024,512]{1,0:T(8,128)(2,1)S(1)} %keys.3.more_ref, ...), custom_call_target="tpu_custom_call" | custom-call | flops 4294967296 | bytes 4194304 | tf_op jit(solution)/shard_map/cross/pallas_call | solution.py:186
  35.4 1.2 %collective-permute-start.6 = (bf16[256,640]{1,0:T(8,128)(2,1)S(1)}, bf16[256,640]{1,0:T(8,128)(2,1)S(1)}, u32[]{:S(2)}, u32[]{:S(2)}) collective-permute-start(bf16[256,640]{1,0:T(8,128)(2,1)S(1)} %get-tuple-element.16), channel_id=1, source_target_pairs={{0,64},{1,17},{8,72},{9,25},{16,80},{17,1},{24,88},{25,9},{32,96},... | collective-permute-start | bytes 983048 | tf_op jit(solution)/shard_map/ppermute | solution.py:360
  36.6 1.2 %collective-permute-start.7 = (bf16[256,640]{1,0:T(8,128)(2,1)S(1)}, bf16[256,640]{1,0:T(8,128)(2,1)S(1)}, u32[]{:S(2)}, u32[]{:S(2)}) collective-permute-start(bf16[256,640]{1,0:T(8,128)(2,1)S(1)} %get-tuple-element.17), channel_id=1, source_target_pairs={{0,32},{1,9},{8,40},{9,17},{16,48},{17,25},{24,56},{25,1},{32,64},... | collective-permute-start | bytes 983048 | tf_op jit(solution)/shard_map/ppermute | solution.py:360
  37.8 3.7 %cross.4 = bf16[256,640]{1,0:T(8,128)(2,1)S(1)} custom-call(s32[6]{0:T(128)S(1)} %stack.55.ids_ref, s32[1024]{0:T(1024)S(1)} %broadcast_select_fusion.cutoff_ref, s32[1024,128]{1,0:T(8,128)S(1)} %broadcast_in_dim.4.cut_ref, bf16[1024,512]{1,0:T(8,128)(2,1)S(1)} %keys.2.k_ref, bf16[1024,512]{1,0:T(8,128)(2,1)S(1)} %keys.3.more_ref, ...), custom_call_target="tpu_custom_call" | custom-call | flops 2147483648 | bytes 4194304 | tf_op jit(solution)/shard_map/cross/pallas_call | solution.py:186
  41.5 1.6 %collective-permute-start.9 = (bf16[256,640]{1,0:T(8,128)(2,1)S(1)}, bf16[256,640]{1,0:T(8,128)(2,1)S(1)}, u32[]{:S(2)}, u32[]{:S(2)}) collective-permute-start(bf16[256,640]{1,0:T(8,128)(2,1)S(1)} %cross.4), channel_id=1, source_target_pairs={{0,96},{1,25},{8,104},{9,1},{16,112},{17,9},{24,120},{25,17},{32,0... | collective-permute-start | bytes 983048 | tf_op jit(solution)/shard_map/ppermute | solution.py:360
  43.1 4.0 %cross.5.d_ref = bf16[256,640]{1,0:T(8,128)(2,1)S(1)} custom-call(s32[6]{0:T(128)S(1)} %stack.55.ids_ref, s32[1024]{0:T(1024)S(1)} %broadcast_select_fusion.cutoff_ref, s32[1024,128]{1,0:T(8,128)S(1)} %broadcast_in_dim.4.cut_ref, bf16[1024,512]{1,0:T(8,128)(2,1)S(1)} %keys.2.k_ref, bf16[1024,512]{1,0:T(8,128)(2,1)S(1)} %keys.3.more_ref, ...), custom_call_target="tpu_custom_call" | custom-call | flops 2147483648 | bytes 4194304 | tf_op jit(solution)/shard_map/cross/pallas_call | solution.py:186
  47.1 0.7 collective-permute-done.9.c_ref
  47.8 1.0 blend.1
  48.8 10.6 %all_to_all.10.parts_ref = bf16[8,32,640]{2,1,0:T(8,128)(2,1)S(1)} all-to-all(bf16[8,32,640]{2,1,0:T(8,128)(2,1)S(1)} %bitcast.21), channel_id=1, replica_groups={{0,4,8,12,16,20,24,28},{1,5,33,37,65,69,97,101},{32,36,40,44,48,52,56,6..., dimensions={0} | all-to-all | bytes 655360 | tf_op jit(solution)/shard_map/all_to_all | solution.py:370
  59.4 0.7 cross_output.1
  60.1 5.1 %collective-permute-start.10 = (bf16[32,2048]{1,0:T(8,128)(2,1)S(1)}, bf16[32,2048]{1,0:T(8,128)(2,1)S(1)}, u32[]{:S(2)}, u32[]{:S(2)}) collective-permute-start(bf16[32,2048]{1,0:T(8,128)(2,1)S(1)} %cross_output.1), channel_id=1, source_target_pairs={{0,1},{1,0},{2,3},{3,2},{4,5},{5,4},{6,7},{7,6},{8,9},{9,8},{10,11... | collective-permute-start | bytes 393224 | tf_op jit(solution)/shard_map/ppermute | solution.py:343
  65.2 1.0 collective-permute-done.10
  66.2 2.7 %collective-permute-start.11 = (bf16[32,2048]{1,0:T(8,128)(2,1)S(1)}, bf16[32,2048]{1,0:T(8,128)(2,1)S(1)}, u32[]{:S(2)}, u32[]{:S(2)}) collective-permute-start(bf16[32,2048]{1,0:T(8,128)(2,1)S(1)} %add_convert_fusion.2.one_ref), channel_id=1, source_target_pairs={{0,2},{2,0},{1,3},{3,1},{4,6},{6,4},{5,7},{7,5},{8,10},{10,8},{9,1... | collective-permute-start | bytes 393224 | tf_op jit(solution)/shard_map/ppermute | solution.py:343
  68.9 3.6 %collective-permute-done.11.two_ref = bf16[32,2048]{1,0:T(8,128)(2,1)S(1)} collective-permute-done((bf16[32,2048]{1,0:T(8,128)(2,1)S(1)}, bf16[32,2048]{1,0:T(8,128)(2,1)S(1)}, u32[]{:S(2)}, u32[]{:S(2)}) %collective-permute-start.11) | collective-permute-done | bytes 131104 | tf_op jit(solution)/shard_map/ppermute | solution.py:343
  72.5 1.8 %self_project.1 = (f32[32,2048]{1,0:T(8,128)S(1)}, bf16[32,384]{1,0:T(8,128)(2,1)S(1)}, bf16[32,384]{1,0:T(8,128)(2,1)S(1)}, bf16[32,384]{1,0:T(8,128)(2,1)S(1)}, bf16[32,384]{1,0:T(8,128)(2,1)S(1)}) custom-call(s32[6]{0:T(128)S(1)} %stack.55.ids_ref, bf16[32,2048]{1,0:T(8,128)(2,1)S(1)} %copy-done.9, bf16[32,2048]{1,0:T(8,128)(2,1)S(1)} %add_convert_fusion.2.one_ref, ...), custom_call_target="tpu_custom_call" | custom-call | tf_op jit(solution)/shard_map/self_project/pallas_call | solution.py:274
  74.4 1.0 collective-permute-start.14
  75.4 1.2 %collective-permute-start.13 = (bf16[32,384]{1,0:T(8,128)(2,1)S(1)}, bf16[32,384]{1,0:T(8,128)(2,1)S(1)}, u32[]{:S(2)}, u32[]{:S(2)}) collective-permute-start(bf16[32,384]{1,0:T(8,128)(2,1)S(1)} %get-tuple-element.21), channel_id=1, source_target_pairs={{0,64},{1,17},{8,72},{9,25},{16,80},{17,1},{24,88},{25,9},{32,96},... | collective-permute-start | bytes 73736 | tf_op jit(solution)/shard_map/ppermute | solution.py:360
  76.5 0.6 collective-permute-done.14.d_ref
  77.2 2.4 %collective-permute-done.13.c_ref = bf16[32,384]{1,0:T(8,128)(2,1)S(1)} collective-permute-done((bf16[32,384]{1,0:T(8,128)(2,1)S(1)}, bf16[32,384]{1,0:T(8,128)(2,1)S(1)}, u32[]{:S(2)}, u32[]{:S(2)}) %collective-permute-start.13) | collective-permute-done | bytes 24608 | tf_op jit(solution)/shard_map/ppermute | solution.py:360
  79.5 0.9 collective-permute-done.12.b_ref
  80.5 9.6 %all_to_all.11.kv_ref = bf16[8,128,256]{2,1,0:T(8,128)(2,1)S(1)} all-to-all(bf16[8,128,256]{2,1,0:T(8,128)(2,1)S(1)} %broadcast_in_dim.5), channel_id=1, replica_groups={{0,4,8,12,16,20,24,28},{1,5,33,37,65,69,97,101},{32,36,40,44,48,52,56,6..., dimensions={0} | all-to-all | bytes 1048576 | tf_op jit(solution)/shard_map/all_to_all | solution.py:370
  90.1 1.1 %self_attend.1 = (bf16[32,128]{1,0:T(8,128)(2,1)S(1)}, bf16[32,128]{1,0:T(8,128)(2,1)S(1)}, bf16[32,128]{1,0:T(8,128)(2,1)S(1)}, bf16[32,128]{1,0:T(8,128)(2,1)S(1)}) custom-call(s32[6]{0:T(128)S(1)} %stack.55.ids_ref, bf16[32,384]{1,0:T(8,128)(2,1)S(1)} %get-tuple-element.19.a_ref, bf16[32,384]{1,0:T(8,128)(2,1)S(1)} %collective-permute-done.12.b_ref, ...), custom_call_target="tpu_custom_call" | custom-call | tf_op jit(solution)/shard_map/self_attend/pallas_call | solution.py:312
  91.2 0.6 collective-permute-start.15
  91.9 0.9 collective-permute-start.16
  92.8 1.3 %collective-permute-done.15.b_ref = bf16[32,128]{1,0:T(8,128)(2,1)S(1)} collective-permute-done((bf16[32,128]{1,0:T(8,128)(2,1)S(1)}, bf16[32,128]{1,0:T(8,128)(2,1)S(1)}, u32[]{:S(2)}, u32[]{:S(2)}) %collective-permute-start.15) | collective-permute-done | bytes 8224 | tf_op jit(solution)/shard_map/ppermute | solution.py:360
  94.1 1.8 %collective-permute-done.16.c_ref = bf16[32,128]{1,0:T(8,128)(2,1)S(1)} collective-permute-done((bf16[32,128]{1,0:T(8,128)(2,1)S(1)}, bf16[32,128]{1,0:T(8,128)(2,1)S(1)}, u32[]{:S(2)}, u32[]{:S(2)}) %collective-permute-start.16) | collective-permute-done | bytes 8224 | tf_op jit(solution)/shard_map/ppermute | solution.py:360
  95.9 0.6 collective-permute-done.17.d_ref
  96.5 1.0 self_output.1
  97.5 5.9 %collective-permute-start.18 = (bf16[32,2048]{1,0:T(8,128)(2,1)S(1)}, bf16[32,2048]{1,0:T(8,128)(2,1)S(1)}, u32[]{:S(2)}, u32[]{:S(2)}) collective-permute-start(bf16[32,2048]{1,0:T(8,128)(2,1)S(1)} %self_output.1), channel_id=1, source_target_pairs={{0,1},{1,0},{2,3},{3,2},{4,5},{5,4},{6,7},{7,6},{8,9},{9,8},{10,11... | collective-permute-start | bytes 393224 | tf_op jit(solution)/shard_map/ppermute | solution.py:343
  103.4 1.0 collective-permute-done.18
  104.4 2.7 %collective-permute-start.19 = (bf16[32,2048]{1,0:T(8,128)(2,1)S(1)}, bf16[32,2048]{1,0:T(8,128)(2,1)S(1)}, u32[]{:S(2)}, u32[]{:S(2)}) collective-permute-start(bf16[32,2048]{1,0:T(8,128)(2,1)S(1)} %add_convert_fusion.1), channel_id=1, source_target_pairs={{0,2},{2,0},{1,3},{3,1},{4,6},{6,4},{5,7},{7,5},{8,10},{10,8},{9,1... | collective-permute-start | bytes 393224 | tf_op jit(solution)/shard_map/ppermute | solution.py:343
  107.1 3.6 %collective-permute-done.19 = bf16[32,2048]{1,0:T(8,128)(2,1)S(1)} collective-permute-done((bf16[32,2048]{1,0:T(8,128)(2,1)S(1)}, bf16[32,2048]{1,0:T(8,128)(2,1)S(1)}, u32[]{:S(2)}, u32[]{:S(2)}) %collective-permute-start.19) | collective-permute-done | bytes 131104 | tf_op jit(solution)/shard_map/ppermute | solution.py:343
  110.7 0.7 add_convert_fusion
  (50 shorter events, 0.8 us)
Async XLA Ops:
  0.0 10.5 %copy-start.1 = (bf16[2048,512]{1,0:T(8,128)(2,1)S(1)}, bf16[2048,512]{1,0:T(8,128)(2,1)}, u32[]{:S(2)}) copy-start(bf16[2048,512]{1,0:T(8,128)(2,1)} %w_ref.4) | copy-start | bytes 6291460
  0.0 1.7 %copy-start.4 = (bf16[2048,512]{1,0:T(8,128)(2,1)S(1)}, bf16[2048,512]{1,0:T(8,128)(2,1)}, u32[]{:S(2)}) copy-start(bf16[2048,512]{1,0:T(8,128)(2,1)} %wq_ref.2) | copy-start | bytes 6291460
  1.7 0.9 copy-start.8
  2.6 2.7 %copy-start.11 = (s32[1024]{0:T(1024)S(1)}, s32[1024]{0:T(1024)}, u32[]{:S(2)}) copy-start(s32[1024]{0:T(1024)} %param.13) | copy-start | bytes 12292
  3.2 3.5 %collective-permute-start = (bf16[32,512]{1,0:T(8,128)(2,1)S(1)}, bf16[32,512]{1,0:T(8,128)(2,1)S(1)}, u32[]{:S(2)}, u32[]{:S(2)}) collective-permute-start(bf16[32,512]{1,0:T(8,128)(2,1)S(1)} %queries.1), channel_id=1, source_target_pairs={{0,4},{4,0},{1,5},{5,1},{2,6},{6,2},{3,7},{7,3},{8,12},{12,8},{9,1... | collective-permute-start | bytes 98312 | tf_op jit(solution)/shard_map/ppermute | solution.py:343
  6.7 9.6 %collective-permute-start.3 = (bf16[64,512]{1,0:T(8,128)(2,1)S(1)}, bf16[64,512]{1,0:T(8,128)(2,1)S(1)}, u32[]{:S(2)}, u32[]{:S(2)}) collective-permute-start(bf16[64,512]{1,0:T(8,128)(2,1)S(1)} %maximum_select_fusion.after_ref), channel_id=1, source_target_pairs={{0,24},{1,97},{8,0},{9,105},{16,8},{17,113},{24,16},{25,121},{32,5... | collective-permute-start | bytes 196616 | tf_op jit(solution)/shard_map/ppermute | solution.py:360
  9.4 6.9 %collective-permute-start.2 = (bf16[64,512]{1,0:T(8,128)(2,1)S(1)}, bf16[64,512]{1,0:T(8,128)(2,1)S(1)}, u32[]{:S(2)}, u32[]{:S(2)}) collective-permute-start(bf16[64,512]{1,0:T(8,128)(2,1)S(1)} %maximum_select_fusion.after_ref), channel_id=1, source_target_pairs={{0,16},{1,65},{8,24},{9,73},{16,0},{17,81},{24,8},{25,89},{32,48},... | collective-permute-start | bytes 196616 | tf_op jit(solution)/shard_map/ppermute | solution.py:360
  9.9 6.4 %collective-permute-start.1 = (bf16[64,512]{1,0:T(8,128)(2,1)S(1)}, bf16[64,512]{1,0:T(8,128)(2,1)S(1)}, u32[]{:S(2)}, u32[]{:S(2)}) collective-permute-start(bf16[64,512]{1,0:T(8,128)(2,1)S(1)} %maximum_select_fusion.after_ref), channel_id=1, source_target_pairs={{0,8},{1,33},{8,16},{9,41},{16,24},{17,49},{24,0},{25,57},{32,40},... | collective-permute-start | bytes 196616 | tf_op jit(solution)/shard_map/ppermute | solution.py:360
  10.5 3.4 %copy-start = (bf16[2048,2048]{1,0:T(8,128)(2,1)S(1)}, bf16[2048,2048]{1,0:T(8,128)(2,1)}, u32[]{:S(2)}) copy-start(bf16[2048,2048]{1,0:T(8,128)(2,1)} %context_ref.5) | copy-start | bytes 25165828
  13.9 7.7 %copy-start.10 = (bf16[2048,512]{1,0:T(8,128)(2,1)S(1)}, bf16[2048,512]{1,0:T(8,128)(2,1)}, u32[]{:S(2)}) copy-start(bf16[2048,512]{1,0:T(8,128)(2,1)} %w_ref.5) | copy-start | bytes 6291460
  16.4 12.0 %collective-permute-start.4 = (bf16[256,512]{1,0:T(8,128)(2,1)S(1)}, bf16[256,512]{1,0:T(8,128)(2,1)S(1)}, u32[]{:S(2)}, u32[]{:S(2)}) collective-permute-start(bf16[256,512]{1,0:T(8,128)(2,1)S(1)} %pad_maximum_fusion.1.after_ref.rest_0_), channel_id=1, source_target_pairs={{0,64},{1,17},{8,72},{9,25},{16,80},{17,1},{24,88},{25,9},{32,96},... | collective-permute-start | bytes 786440 | tf_op jit(solution)/shard_map/ppermute | solution.py:360
  20.1 8.3 %collective-permute-start.5 = (bf16[256,512]{1,0:T(8,128)(2,1)S(1)}, bf16[256,512]{1,0:T(8,128)(2,1)S(1)}, u32[]{:S(2)}, u32[]{:S(2)}) collective-permute-start(bf16[256,512]{1,0:T(8,128)(2,1)S(1)} %pad_maximum_fusion.1.after_ref.rest_0_), channel_id=1, source_target_pairs={{0,96},{1,25},{8,104},{9,1},{16,112},{17,9},{24,120},{25,17},{32,0... | collective-permute-start | bytes 786440 | tf_op jit(solution)/shard_map/ppermute | solution.py:360
  20.6 17.2 %collective-permute-start.8 = (bf16[256,512]{1,0:T(8,128)(2,1)S(1)}, bf16[256,512]{1,0:T(8,128)(2,1)S(1)}, u32[]{:S(2)}, u32[]{:S(2)}) collective-permute-start(bf16[256,512]{1,0:T(8,128)(2,1)S(1)} %pad_maximum_fusion.1.after_ref.rest_0_), channel_id=1, source_target_pairs={{0,32},{1,9},{8,40},{9,17},{16,48},{17,25},{24,56},{25,1},{32,64},... | collective-permute-start | bytes 786440 | tf_op jit(solution)/shard_map/ppermute | solution.py:360
  35.4 11.6 %collective-permute-start.6 = (bf16[256,640]{1,0:T(8,128)(2,1)S(1)}, bf16[256,640]{1,0:T(8,128)(2,1)S(1)}, u32[]{:S(2)}, u32[]{:S(2)}) collective-permute-start(bf16[256,640]{1,0:T(8,128)(2,1)S(1)} %get-tuple-element.16), channel_id=1, source_target_pairs={{0,64},{1,17},{8,72},{9,25},{16,80},{17,1},{24,88},{25,9},{32,96},... | collective-permute-start | bytes 983048 | tf_op jit(solution)/shard_map/ppermute | solution.py:360
  36.6 10.5 %collective-permute-start.7 = (bf16[256,640]{1,0:T(8,128)(2,1)S(1)}, bf16[256,640]{1,0:T(8,128)(2,1)S(1)}, u32[]{:S(2)}, u32[]{:S(2)}) collective-permute-start(bf16[256,640]{1,0:T(8,128)(2,1)S(1)} %get-tuple-element.17), channel_id=1, source_target_pairs={{0,32},{1,9},{8,40},{9,17},{16,48},{17,25},{24,56},{25,1},{32,64},... | collective-permute-start | bytes 983048 | tf_op jit(solution)/shard_map/ppermute | solution.py:360
  41.5 6.3 %collective-permute-start.9 = (bf16[256,640]{1,0:T(8,128)(2,1)S(1)}, bf16[256,640]{1,0:T(8,128)(2,1)S(1)}, u32[]{:S(2)}, u32[]{:S(2)}) collective-permute-start(bf16[256,640]{1,0:T(8,128)(2,1)S(1)} %cross.4), channel_id=1, source_target_pairs={{0,96},{1,25},{8,104},{9,1},{16,112},{17,9},{24,120},{25,17},{32,0... | collective-permute-start | bytes 983048 | tf_op jit(solution)/shard_map/ppermute | solution.py:360
  43.1 29.4 %copy-start.6 = (bf16[2048,512]{1,0:T(8,128)(2,1)S(1)}, bf16[2048,512]{1,0:T(8,128)(2,1)}, u32[]{:S(2)}) copy-start(bf16[2048,512]{1,0:T(8,128)(2,1)} %wk_ref.1) | copy-start | bytes 6291460
  43.1 29.4 %copy-start.7 = (bf16[2048,512]{1,0:T(8,128)(2,1)S(1)}, bf16[2048,512]{1,0:T(8,128)(2,1)}, u32[]{:S(2)}) copy-start(bf16[2048,512]{1,0:T(8,128)(2,1)} %wv_ref.1) | copy-start | bytes 6291460
  47.1 12.3 %copy-start.2 = (bf16[512,2048]{1,0:T(8,128)(2,1)S(1)}, bf16[512,2048]{1,0:T(8,128)(2,1)}, u32[]{:S(2)}) copy-start(bf16[512,2048]{1,0:T(8,128)(2,1)} %wo_ref.2) | copy-start | bytes 6291460
  48.8 23.8 %copy-start.5 = (bf16[2048,512]{1,0:T(8,128)(2,1)S(1)}, bf16[2048,512]{1,0:T(8,128)(2,1)}, u32[]{:S(2)}) copy-start(bf16[2048,512]{1,0:T(8,128)(2,1)} %wq_ref.3) | copy-start | bytes 6291460
  48.8 23.7 %copy-start.9 = (bf16[32,2048]{1,0:T(8,128)(2,1)S(1)}, bf16[32,2048]{1,0:T(8,128)(2,1)}, u32[]{:S(2)}) copy-start(bf16[32,2048]{1,0:T(8,128)(2,1)} %latent_ref.3) | copy-start | bytes 393220
  60.1 6.1 %collective-permute-start.10 = (bf16[32,2048]{1,0:T(8,128)(2,1)S(1)}, bf16[32,2048]{1,0:T(8,128)(2,1)S(1)}, u32[]{:S(2)}, u32[]{:S(2)}) collective-permute-start(bf16[32,2048]{1,0:T(8,128)(2,1)S(1)} %cross_output.1), channel_id=1, source_target_pairs={{0,1},{1,0},{2,3},{3,2},{4,5},{5,4},{6,7},{7,6},{8,9},{9,8},{10,11... | collective-permute-start | bytes 393224 | tf_op jit(solution)/shard_map/ppermute | solution.py:343
  66.2 6.3 %collective-permute-start.11 = (bf16[32,2048]{1,0:T(8,128)(2,1)S(1)}, bf16[32,2048]{1,0:T(8,128)(2,1)S(1)}, u32[]{:S(2)}, u32[]{:S(2)}) collective-permute-start(bf16[32,2048]{1,0:T(8,128)(2,1)S(1)} %add_convert_fusion.2.one_ref), channel_id=1, source_target_pairs={{0,2},{2,0},{1,3},{3,1},{4,6},{6,4},{5,7},{7,5},{8,10},{10,8},{9,1... | collective-permute-start | bytes 393224 | tf_op jit(solution)/shard_map/ppermute | solution.py:343
  74.4 22.1 %copy-start.3 = (bf16[512,2048]{1,0:T(8,128)(2,1)S(1)}, bf16[512,2048]{1,0:T(8,128)(2,1)}, u32[]{:S(2)}) copy-start(bf16[512,2048]{1,0:T(8,128)(2,1)} %wo_ref.3) | copy-start | bytes 6291460
  74.4 2.7 %collective-permute-start.14 = (bf16[32,384]{1,0:T(8,128)(2,1)S(1)}, bf16[32,384]{1,0:T(8,128)(2,1)S(1)}, u32[]{:S(2)}, u32[]{:S(2)}) collective-permute-start(bf16[32,384]{1,0:T(8,128)(2,1)S(1)} %get-tuple-element.22), channel_id=1, source_target_pairs={{0,96},{1,25},{8,104},{9,1},{16,112},{17,9},{24,120},{25,17},{32,0... | collective-permute-start | bytes 73736 | tf_op jit(solution)/shard_map/ppermute | solution.py:360
  75.4 4.2 %collective-permute-start.13 = (bf16[32,384]{1,0:T(8,128)(2,1)S(1)}, bf16[32,384]{1,0:T(8,128)(2,1)S(1)}, u32[]{:S(2)}, u32[]{:S(2)}) collective-permute-start(bf16[32,384]{1,0:T(8,128)(2,1)S(1)} %get-tuple-element.21), channel_id=1, source_target_pairs={{0,64},{1,17},{8,72},{9,25},{16,80},{17,1},{24,88},{25,9},{32,96},... | collective-permute-start | bytes 73736 | tf_op jit(solution)/shard_map/ppermute | solution.py:360
  76.5 3.9 %collective-permute-start.12 = (bf16[32,384]{1,0:T(8,128)(2,1)S(1)}, bf16[32,384]{1,0:T(8,128)(2,1)S(1)}, u32[]{:S(2)}, u32[]{:S(2)}) collective-permute-start(bf16[32,384]{1,0:T(8,128)(2,1)S(1)} %get-tuple-element.20), channel_id=1, source_target_pairs={{0,32},{1,9},{8,40},{9,17},{16,48},{17,25},{24,56},{25,1},{32,64},... | collective-permute-start | bytes 73736 | tf_op jit(solution)/shard_map/ppermute | solution.py:360
  91.2 2.9 %collective-permute-start.15 = (bf16[32,128]{1,0:T(8,128)(2,1)S(1)}, bf16[32,128]{1,0:T(8,128)(2,1)S(1)}, u32[]{:S(2)}, u32[]{:S(2)}) collective-permute-start(bf16[32,128]{1,0:T(8,128)(2,1)S(1)} %get-tuple-element.24), channel_id=1, source_target_pairs={{0,96},{1,25},{8,104},{9,1},{16,112},{17,9},{24,120},{25,17},{32,0... | collective-permute-start | bytes 24584 | tf_op jit(solution)/shard_map/ppermute | solution.py:360
  91.9 4.0 %collective-permute-start.16 = (bf16[32,128]{1,0:T(8,128)(2,1)S(1)}, bf16[32,128]{1,0:T(8,128)(2,1)S(1)}, u32[]{:S(2)}, u32[]{:S(2)}) collective-permute-start(bf16[32,128]{1,0:T(8,128)(2,1)S(1)} %get-tuple-element.25), channel_id=1, source_target_pairs={{0,64},{1,17},{8,72},{9,25},{16,80},{17,1},{24,88},{25,9},{32,96},... | collective-permute-start | bytes 24584 | tf_op jit(solution)/shard_map/ppermute | solution.py:360
  92.8 3.7 %collective-permute-start.17 = (bf16[32,128]{1,0:T(8,128)(2,1)S(1)}, bf16[32,128]{1,0:T(8,128)(2,1)S(1)}, u32[]{:S(2)}, u32[]{:S(2)}) collective-permute-start(bf16[32,128]{1,0:T(8,128)(2,1)S(1)} %get-tuple-element.26), channel_id=1, source_target_pairs={{0,32},{1,9},{8,40},{9,17},{16,48},{17,25},{24,56},{25,1},{32,64},... | collective-permute-start | bytes 24584 | tf_op jit(solution)/shard_map/ppermute | solution.py:360
  97.5 6.8 %collective-permute-start.18 = (bf16[32,2048]{1,0:T(8,128)(2,1)S(1)}, bf16[32,2048]{1,0:T(8,128)(2,1)S(1)}, u32[]{:S(2)}, u32[]{:S(2)}) collective-permute-start(bf16[32,2048]{1,0:T(8,128)(2,1)S(1)} %self_output.1), channel_id=1, source_target_pairs={{0,1},{1,0},{2,3},{3,2},{4,5},{5,4},{6,7},{7,6},{8,9},{9,8},{10,11... | collective-permute-start | bytes 393224 | tf_op jit(solution)/shard_map/ppermute | solution.py:343
  104.4 6.3 %collective-permute-start.19 = (bf16[32,2048]{1,0:T(8,128)(2,1)S(1)}, bf16[32,2048]{1,0:T(8,128)(2,1)S(1)}, u32[]{:S(2)}, u32[]{:S(2)}) collective-permute-start(bf16[32,2048]{1,0:T(8,128)(2,1)S(1)} %add_convert_fusion.1), channel_id=1, source_target_pairs={{0,2},{2,0},{1,3},{3,1},{4,6},{6,4},{5,7},{7,5},{8,10},{10,8},{9,1... | collective-permute-start | bytes 393224 | tf_op jit(solution)/shard_map/ppermute | solution.py:343
where the time goes:
time: 112 us; the launch traced here: 111 us
  starting transfers between devices  35.1 us (31%)
  Pallas kernels  29.9 us (27%)
  blocking collectives  20.2 us (18%)
  waiting for transfers between devices  18.5 us (17%)
  local copies, waits for them, and re-layouts  6.58 us (6%)
    all_to_all x2, blocking collectives, exchanged(): return lax.all_to_all(tensor, WHOLE, 0, 0, axis_index_groups=groups)  20.2 us
    ppermute x5, starting transfers between devices, moved(): lax.ppermute(tensor, axis, [(i, (i + offset) % size) for i in range(size)])  18.5 us
    ppermute x15, starting transfers between devices, turned(): return lax.ppermute(tensor, PLANE, pairs)  16.6 us
    pallas_call x3, Pallas kernels, cross_attend(): pl.pallas_call(functools.partial(cross_kernel, offsets), out_shape=[shape...  14.5 us
    ppermute x5, waiting for transfers between devices, moved(): lax.ppermute(tensor, axis, [(i, (i + offset) % size) for i in range(size)])  10.2 us
    pallas_call x3, Pallas kernels, project_context(): pl.pallas_call(functools.partial(context_kernel, first, min(512, rows)),...  9.18 us
    ppermute x15, waiting for transfers between devices, turned(): return lax.ppermute(tensor, PLANE, pairs)  8.3 us
    unnamed x24, local copies, waits for them, and re-layouts  6.07 us
  transfers between devices with their start and end apart: 20, of which 12 were waited for; matrix products, arithmetic and copies ran while one was open for 0% of the time, Pallas kernels for 21%

commit v1 on v0

--- a/solution.py
+++ b/solution.py
@@ -17,6 +17,7 @@
 BF16 = jnp.bfloat16
 
 VMEM = pl.BlockSpec(memory_space=pltpu.VMEM)
+HBM = pl.BlockSpec(memory_space=pltpu.HBM)
 SMEM = pl.BlockSpec(memory_space=pltpu.SMEM)
 
 
@@ -44,25 +45,47 @@
     return lax.rsqrt(jnp.mean(tile * tile, axis=-1, keepdims=True) + EPSILON)
 
 
-def query_kernel(latent_ref, wq_ref, out_ref):
-    tile = latent_ref[...].astype(F32)
+def query_kernel(latent_ref, wq_ref, out_ref, latent, weight, sems):
+    pieces = weight.shape[0]
+    depth = weight.shape[1]
+    first = pltpu.make_async_copy(latent_ref, latent, sems.at[pieces])
+    copies = [
+        pltpu.make_async_copy(wq_ref.at[pl.ds(i * depth, depth)], weight.at[i], sems.at[i])
+        for i in range(pieces)
+    ]
+    for copy in [first] + copies:
+        copy.start()
+    first.wait()
+    tile = latent[...].astype(F32)
     normed = (tile * inv_rms(tile)).astype(BF16)
-    factor = HEAD_DIM ** (-0.5) * LOG2E
-    out_ref[...] = (dot(normed, wq_ref[...]) * factor).astype(BF16)
+    total = jnp.zeros(out_ref.shape, F32)
+    for i, copy in enumerate(copies):
+        copy.wait()
+        total += dot(normed[:, i * depth : (i + 1) * depth], weight[i])
+    out_ref[...] = (total * (HEAD_DIM ** (-0.5) * LOG2E)).astype(BF16)
 
 
 def project_queries(latent_in, wq):
     rows, width = latent_in.shape
     cols = wq.shape[1]
+    pieces = 4
     return pl.pallas_call(
         query_kernel,
         out_shape=shape_of((rows, cols)),
-        in_specs=[VMEM, VMEM],
+        in_specs=[HBM, HBM],
         out_specs=VMEM,
-        compiler_params=params(8),
+        scratch_shapes=[
+            pltpu.VMEM((rows, width), BF16),
+            pltpu.VMEM((pieces, width // pieces, cols), BF16),
+            pltpu.SemaphoreType.DMA((pieces + 1,)),
+        ],
+        compiler_params=params(20),
         cost_estimate=cost(2 * rows * width * cols, 2 * width * cols),
         name="queries",
-    )(latent_in, wq)
+    )(
+        pltpu.with_memory_space_constraint(latent_in, pltpu.HBM),
+        pltpu.with_memory_space_constraint(wq, pltpu.HBM),
+    )
 
 
 def context_kernel(first, step, context_ref, w_ref, after_ref, out_ref):

time: 112 us -> 111 us (level)
  local copies, waits for them, and re-layouts: 6.58 us -> 3.93 us
  Pallas kernels: 29.9 us -> 31.3 us
  blocking collectives: 20.2 us -> 21.4 us
    unnamed x24 -> x20, local copies, waits for them, and re-layouts: 6.07 us -> 3.43 us
    pallas_call x1, Pallas kernels: 0.52 us -> 1.97 us  [project_queries(): pl.pallas_call(query_kernel, out_shape=shape_of((rows, cols)), in_specs=[...]
    all_to_all x2, blocking collectives: 20.2 us -> 21.4 us  [exchanged(): return lax.all_to_all(tensor, WHOLE, 0, 0, axis_index_groups=groups)]
where the time goes in v1:
time: 111 us
  starting transfers between devices  35 us (32%)
  Pallas kernels  31.3 us (28%)
  blocking collectives  21.4 us (19%)
  waiting for transfers between devices  18.1 us (16%)
  local copies, waits for them, and re-layouts  3.93 us (4%)
    all_to_all x2, blocking collectives, exchanged(): return lax.all_to_all(tensor, WHOLE, 0, 0, axis_index_groups=groups)  21.4 us
    ppermute x5, starting transfers between devices, moved(): lax.ppermute(tensor, axis, [(i, (i + offset) % size) for i in range(size)])  18.5 us
    ppermute x15, starting transfers between devices, turned(): return lax.ppermute(tensor, PLANE, pairs)  16.6 us
    pallas_call x3, Pallas kernels, cross_attend(): pl.pallas_call(functools.partial(cross_kernel, offsets), out_shape=[shape...  14.5 us
    ppermute x5, waiting for transfers between devices, moved(): lax.ppermute(tensor, axis, [(i, (i + offset) % size) for i in range(size)])  9.96 us
    pallas_call x3, Pallas kernels, project_context(): pl.pallas_call(functools.partial(context_kernel, first, min(512, rows)),...  9.18 us
    ppermute x15, waiting for transfers between devices, turned(): return lax.ppermute(tensor, PLANE, pairs)  8.14 us
    unnamed x20, local copies, waits for them, and re-layouts  3.43 us
  transfers between devices with their start and end apart: 20, of which 12 were waited for; matrix products, arithmetic and copies ran while one was open for 0% of the time, Pallas kernels for 21%

profile of v1, /device:TPU:1, one launch (start us, length us, event | category | flops | bytes accessed | tf_op | source)
XLA Modules:
  0.0 110.9 jit_solution(9599371273083907935)
XLA Ops:
  0.0 2.0 %queries.1 = bf16[32,512]{1,0:T(8,128)(2,1)S(1)} custom-call(bf16[32,2048]{1,0:T(8,128)(2,1)} %latent_ref.3, bf16[2048,512]{1,0:T(8,128)(2,1)} %wq_ref.2), custom_call_target="tpu_custom_call" | custom-call | flops 67108864 | bytes 2097152 | tf_op jit(solution)/shard_map/queries/pallas_call | solution.py:72
  2.0 2.2 %collective-permute-start = (bf16[32,512]{1,0:T(8,128)(2,1)S(1)}, bf16[32,512]{1,0:T(8,128)(2,1)S(1)}, u32[]{:S(2)}, u32[]{:S(2)}) collective-permute-start(bf16[32,512]{1,0:T(8,128)(2,1)S(1)} %queries.1), channel_id=1, source_target_pairs={{0,4},{4,0},{1,5},{5,1},{2,6},{6,2},{3,7},{7,3},{8,12},{12,8},{9,1... | collective-permute-start | bytes 98312 | tf_op jit(solution)/shard_map/ppermute | solution.py:366
  4.4 1.0 collective-permute-done
  5.5 2.7 %collective-permute-start.3 = (bf16[64,512]{1,0:T(8,128)(2,1)S(1)}, bf16[64,512]{1,0:T(8,128)(2,1)S(1)}, u32[]{:S(2)}, u32[]{:S(2)}) collective-permute-start(bf16[64,512]{1,0:T(8,128)(2,1)S(1)} %maximum_select_fusion.after_ref), channel_id=1, source_target_pairs={{0,24},{1,97},{8,0},{9,105},{16,8},{17,113},{24,16},{25,121},{32,5... | collective-permute-start | bytes 196616 | tf_op jit(solution)/shard_map/ppermute | solution.py:383
  8.2 0.5 collective-permute-start.2
  8.7 0.6 collective-permute-start.1
  9.4 3.4 %copy-done = bf16[2048,2048]{1,0:T(8,128)(2,1)S(1)} copy-done((bf16[2048,2048]{1,0:T(8,128)(2,1)S(1)}, bf16[2048,2048]{1,0:T(8,128)(2,1)}, u32[]{:S(2)}) %copy-start) | copy-done | bytes 8388632
  12.7 2.3 %keys.2.k_ref = bf16[1024,512]{1,0:T(8,128)(2,1)S(1)} custom-call(bf16[2048,2048]{1,0:T(8,128)(2,1)S(1)} %copy-done, bf16[2048,512]{1,0:T(8,128)(2,1)S(1)} %copy-done.1, bf16[64,512]{1,0:T(8,128)(2,1)S(1)} %maximum_select_fusion.after_ref), custom_call_target="tpu_custom_call" | custom-call | flops 2147483648 | bytes 6291456 | tf_op jit(solution)/shard_map/keys/pallas_call | solution.py:105
  15.2 3.7 %collective-permute-start.4 = (bf16[256,512]{1,0:T(8,128)(2,1)S(1)}, bf16[256,512]{1,0:T(8,128)(2,1)S(1)}, u32[]{:S(2)}, u32[]{:S(2)}) collective-permute-start(bf16[256,512]{1,0:T(8,128)(2,1)S(1)} %pad_maximum_fusion.1.after_ref.rest_0_), channel_id=1, source_target_pairs={{0,64},{1,17},{8,72},{9,25},{16,80},{17,1},{24,88},{25,9},{32,96},... | collective-permute-start | bytes 786440 | tf_op jit(solution)/shard_map/ppermute | solution.py:383
  18.9 0.4 collective-permute-start.5
  19.4 1.0 collective-permute-start.8
  20.4 4.5 %values.1.v_ref = bf16[2048,512]{1,0:T(8,128)(2,1)S(1)} custom-call(bf16[2048,2048]{1,0:T(8,128)(2,1)S(1)} %copy-done, bf16[2048,512]{1,0:T(8,128)(2,1)S(1)} %copy-done.8, bf16[256,512]{1,0:T(8,128)(2,1)S(1)} %pad_maximum_fusion.1.after_ref.rest_0_), custom_call_target="tpu_custom_call" | custom-call | flops 4294967296 | bytes 10485760 | tf_op jit(solution)/shard_map/values/pallas_call | solution.py:105
  24.9 2.3 %keys.3.more_ref = bf16[1024,512]{1,0:T(8,128)(2,1)S(1)} custom-call(bf16[2048,2048]{1,0:T(8,128)(2,1)S(1)} %copy-done, bf16[2048,512]{1,0:T(8,128)(2,1)S(1)} %copy-done.1, bf16[256,512]{1,0:T(8,128)(2,1)S(1)} %pad_maximum_fusion.1.after_ref.rest_0_), custom_call_target="tpu_custom_call" | custom-call | flops 2147483648 | bytes 6291456 | tf_op jit(solution)/shard_map/keys/pallas_call | solution.py:105
  27.3 0.2 broadcast_in_dim.4.cut_ref
  27.5 6.8 %cross.3 = (bf16[256,640]{1,0:T(8,128)(2,1)S(1)}, bf16[256,640]{1,0:T(8,128)(2,1)S(1)}) custom-call(s32[6]{0:T(128)S(1)} %stack.55.ids_ref, s32[1024]{0:T(1024)S(1)} %broadcast_select_fusion.cutoff_ref, s32[1024,128]{1,0:T(8,128)S(1)} %broadcast_in_dim.4.cut_ref, bf16[1024,512]{1,0:T(8,128)(2,1)S(1)} %keys.2.k_ref, bf16[1024,512]{1,0:T(8,128)(2,1)S(1)} %keys.3.more_ref, ...), custom_call_target="tpu_custom_call" | custom-call | flops 4294967296 | bytes 4194304 | tf_op jit(solution)/shard_map/cross/pallas_call | solution.py:209
  34.2 1.1 %collective-permute-start.6 = (bf16[256,640]{1,0:T(8,128)(2,1)S(1)}, bf16[256,640]{1,0:T(8,128)(2,1)S(1)}, u32[]{:S(2)}, u32[]{:S(2)}) collective-permute-start(bf16[256,640]{1,0:T(8,128)(2,1)S(1)} %get-tuple-element.16), channel_id=1, source_target_pairs={{0,64},{1,17},{8,72},{9,25},{16,80},{17,1},{24,88},{25,9},{32,96},... | collective-permute-start | bytes 983048 | tf_op jit(solution)/shard_map/ppermute | solution.py:383
  35.4 1.2 %collective-permute-start.7 = (bf16[256,640]{1,0:T(8,128)(2,1)S(1)}, bf16[256,640]{1,0:T(8,128)(2,1)S(1)}, u32[]{:S(2)}, u32[]{:S(2)}) collective-permute-start(bf16[256,640]{1,0:T(8,128)(2,1)S(1)} %get-tuple-element.17), channel_id=1, source_target_pairs={{0,32},{1,9},{8,40},{9,17},{16,48},{17,25},{24,56},{25,1},{32,64},... | collective-permute-start | bytes 983048 | tf_op jit(solution)/shard_map/ppermute | solution.py:383
  36.6 3.7 %cross.4 = bf16[256,640]{1,0:T(8,128)(2,1)S(1)} custom-call(s32[6]{0:T(128)S(1)} %stack.55.ids_ref, s32[1024]{0:T(1024)S(1)} %broadcast_select_fusion.cutoff_ref, s32[1024,128]{1,0:T(8,128)S(1)} %broadcast_in_dim.4.cut_ref, bf16[1024,512]{1,0:T(8,128)(2,1)S(1)} %keys.2.k_ref, bf16[1024,512]{1,0:T(8,128)(2,1)S(1)} %keys.3.more_ref, ...), custom_call_target="tpu_custom_call" | custom-call | flops 2147483648 | bytes 4194304 | tf_op jit(solution)/shard_map/cross/pallas_call | solution.py:209
  40.3 1.6 %collective-permute-start.9 = (bf16[256,640]{1,0:T(8,128)(2,1)S(1)}, bf16[256,640]{1,0:T(8,128)(2,1)S(1)}, u32[]{:S(2)}, u32[]{:S(2)}) collective-permute-start(bf16[256,640]{1,0:T(8,128)(2,1)S(1)} %cross.4), channel_id=1, source_target_pairs={{0,96},{1,25},{8,104},{9,1},{16,112},{17,9},{24,120},{25,17},{32,0... | collective-permute-start | bytes 983048 | tf_op jit(solution)/shard_map/ppermute | solution.py:383
  41.9 4.0 %cross.5.d_ref = bf16[256,640]{1,0:T(8,128)(2,1)S(1)} custom-call(s32[6]{0:T(128)S(1)} %stack.55.ids_ref, s32[1024]{0:T(1024)S(1)} %broadcast_select_fusion.cutoff_ref, s32[1024,128]{1,0:T(8,128)S(1)} %broadcast_in_dim.4.cut_ref, bf16[1024,512]{1,0:T(8,128)(2,1)S(1)} %keys.2.k_ref, bf16[1024,512]{1,0:T(8,128)(2,1)S(1)} %keys.3.more_ref, ...), custom_call_target="tpu_custom_call" | custom-call | flops 2147483648 | bytes 4194304 | tf_op jit(solution)/shard_map/cross/pallas_call | solution.py:209
  45.9 0.7 collective-permute-done.9.c_ref
  46.6 1.0 blend.1
  47.6 10.6 %all_to_all.10.parts_ref = bf16[8,32,640]{2,1,0:T(8,128)(2,1)S(1)} all-to-all(bf16[8,32,640]{2,1,0:T(8,128)(2,1)S(1)} %bitcast.21), channel_id=1, replica_groups={{0,4,8,12,16,20,24,28},{1,5,33,37,65,69,97,101},{32,36,40,44,48,52,56,6..., dimensions={0} | all-to-all | bytes 655360 | tf_op jit(solution)/shard_map/all_to_all | solution.py:393
  58.2 0.7 cross_output.1
  58.9 5.1 %collective-permute-start.10 = (bf16[32,2048]{1,0:T(8,128)(2,1)S(1)}, bf16[32,2048]{1,0:T(8,128)(2,1)S(1)}, u32[]{:S(2)}, u32[]{:S(2)}) collective-permute-start(bf16[32,2048]{1,0:T(8,128)(2,1)S(1)} %cross_output.1), channel_id=1, source_target_pairs={{0,1},{1,0},{2,3},{3,2},{4,5},{5,4},{6,7},{7,6},{8,9},{9,8},{10,11... | collective-permute-start | bytes 393224 | tf_op jit(solution)/shard_map/ppermute | solution.py:366
  64.0 1.0 collective-permute-done.10
  65.0 2.7 %collective-permute-start.11 = (bf16[32,2048]{1,0:T(8,128)(2,1)S(1)}, bf16[32,2048]{1,0:T(8,128)(2,1)S(1)}, u32[]{:S(2)}, u32[]{:S(2)}) collective-permute-start(bf16[32,2048]{1,0:T(8,128)(2,1)S(1)} %add_convert_fusion.2.one_ref), channel_id=1, source_target_pairs={{0,2},{2,0},{1,3},{3,1},{4,6},{6,4},{5,7},{7,5},{8,10},{10,8},{9,1... | collective-permute-start | bytes 393224 | tf_op jit(solution)/shard_map/ppermute | solution.py:366
  67.7 3.6 %collective-permute-done.11.two_ref = bf16[32,2048]{1,0:T(8,128)(2,1)S(1)} collective-permute-done((bf16[32,2048]{1,0:T(8,128)(2,1)S(1)}, bf16[32,2048]{1,0:T(8,128)(2,1)S(1)}, u32[]{:S(2)}, u32[]{:S(2)}) %collective-permute-start.11) | collective-permute-done | bytes 131104 | tf_op jit(solution)/shard_map/ppermute | solution.py:366
  71.3 1.8 %self_project.1 = (f32[32,2048]{1,0:T(8,128)S(1)}, bf16[32,384]{1,0:T(8,128)(2,1)S(1)}, bf16[32,384]{1,0:T(8,128)(2,1)S(1)}, bf16[32,384]{1,0:T(8,128)(2,1)S(1)}, bf16[32,384]{1,0:T(8,128)(2,1)S(1)}) custom-call(s32[6]{0:T(128)S(1)} %stack.55.ids_ref, bf16[32,2048]{1,0:T(8,128)(2,1)S(1)} %copy-done.7, bf16[32,2048]{1,0:T(8,128)(2,1)S(1)} %add_convert_fusion.2.one_ref, ...), custom_call_target="tpu_custom_call" | custom-call | tf_op jit(solution)/shard_map/self_project/pallas_call | solution.py:297
  73.2 1.0 collective-permute-start.14
  74.1 1.2 %collective-permute-start.13 = (bf16[32,384]{1,0:T(8,128)(2,1)S(1)}, bf16[32,384]{1,0:T(8,128)(2,1)S(1)}, u32[]{:S(2)}, u32[]{:S(2)}) collective-permute-start(bf16[32,384]{1,0:T(8,128)(2,1)S(1)} %get-tuple-element.21), channel_id=1, source_target_pairs={{0,64},{1,17},{8,72},{9,25},{16,80},{17,1},{24,88},{25,9},{32,96},... | collective-permute-start | bytes 73736 | tf_op jit(solution)/shard_map/ppermute | solution.py:383
  75.3 0.6 collective-permute-done.14.d_ref
  75.9 2.4 %collective-permute-done.13.c_ref = bf16[32,384]{1,0:T(8,128)(2,1)S(1)} collective-permute-done((bf16[32,384]{1,0:T(8,128)(2,1)S(1)}, bf16[32,384]{1,0:T(8,128)(2,1)S(1)}, u32[]{:S(2)}, u32[]{:S(2)}) %collective-permute-start.13) | collective-permute-done | bytes 24608 | tf_op jit(solution)/shard_map/ppermute | solution.py:383
  78.3 0.9 collective-permute-done.12.b_ref
  79.3 10.9 %all_to_all.11.kv_ref = bf16[8,128,256]{2,1,0:T(8,128)(2,1)S(1)} all-to-all(bf16[8,128,256]{2,1,0:T(8,128)(2,1)S(1)} %broadcast_in_dim.5), channel_id=1, replica_groups={{0,4,8,12,16,20,24,28},{1,5,33,37,65,69,97,101},{32,36,40,44,48,52,56,6..., dimensions={0} | all-to-all | bytes 1048576 | tf_op jit(solution)/shard_map/all_to_all | solution.py:393
  90.1 1.1 %self_attend.1 = (bf16[32,128]{1,0:T(8,128)(2,1)S(1)}, bf16[32,128]{1,0:T(8,128)(2,1)S(1)}, bf16[32,128]{1,0:T(8,128)(2,1)S(1)}, bf16[32,128]{1,0:T(8,128)(2,1)S(1)}) custom-call(s32[6]{0:T(128)S(1)} %stack.55.ids_ref, bf16[32,384]{1,0:T(8,128)(2,1)S(1)} %get-tuple-element.19.a_ref, bf16[32,384]{1,0:T(8,128)(2,1)S(1)} %collective-permute-done.12.b_ref, ...), custom_call_target="tpu_custom_call" | custom-call | tf_op jit(solution)/shard_map/self_attend/pallas_call | solution.py:335
  91.3 0.4 collective-permute-start.15
  91.7 0.9 collective-permute-start.16
  92.7 0.2 collective-permute-start.17
  92.8 1.0 collective-permute-done.15.b_ref
  93.9 1.9 %collective-permute-done.16.c_ref = bf16[32,128]{1,0:T(8,128)(2,1)S(1)} collective-permute-done((bf16[32,128]{1,0:T(8,128)(2,1)S(1)}, bf16[32,128]{1,0:T(8,128)(2,1)S(1)}, u32[]{:S(2)}, u32[]{:S(2)}) %collective-permute-start.16) | collective-permute-done | bytes 8224 | tf_op jit(solution)/shard_map/ppermute | solution.py:383
  95.7 0.6 collective-permute-done.17.d_ref
  96.4 1.0 self_output.1
  97.4 5.5 %collective-permute-start.18 = (bf16[32,2048]{1,0:T(8,128)(2,1)S(1)}, bf16[32,2048]{1,0:T(8,128)(2,1)S(1)}, u32[]{:S(2)}, u32[]{:S(2)}) collective-permute-start(bf16[32,2048]{1,0:T(8,128)(2,1)S(1)} %self_output.1), channel_id=1, source_target_pairs={{0,1},{1,0},{2,3},{3,2},{4,5},{5,4},{6,7},{7,6},{8,9},{9,8},{10,11... | collective-permute-start | bytes 393224 | tf_op jit(solution)/shard_map/ppermute | solution.py:366
  102.9 1.0 collective-permute-done.18
  103.9 3.0 %collective-permute-start.19 = (bf16[32,2048]{1,0:T(8,128)(2,1)S(1)}, bf16[32,2048]{1,0:T(8,128)(2,1)S(1)}, u32[]{:S(2)}, u32[]{:S(2)}) collective-permute-start(bf16[32,2048]{1,0:T(8,128)(2,1)S(1)} %add_convert_fusion.1), channel_id=1, source_target_pairs={{0,2},{2,0},{1,3},{3,1},{4,6},{6,4},{5,7},{7,5},{8,10},{10,8},{9,1... | collective-permute-start | bytes 393224 | tf_op jit(solution)/shard_map/ppermute | solution.py:366
  106.9 3.3 %collective-permute-done.19 = bf16[32,2048]{1,0:T(8,128)(2,1)S(1)} collective-permute-done((bf16[32,2048]{1,0:T(8,128)(2,1)S(1)}, bf16[32,2048]{1,0:T(8,128)(2,1)S(1)}, u32[]{:S(2)}, u32[]{:S(2)}) %collective-permute-start.19) | collective-permute-done | bytes 131104 | tf_op jit(solution)/shard_map/ppermute | solution.py:366
  110.2 0.7 add_convert_fusion
  (46 shorter events, 0.6 us)
Async XLA Ops:
  0.0 4.2 %copy-start.9 = (s32[1024]{0:T(1024)S(1)}, s32[1024]{0:T(1024)}, u32[]{:S(2)}) copy-start(s32[1024]{0:T(1024)} %param.13) | copy-start | bytes 12292
  0.0 9.3 %copy-start.1 = (bf16[2048,512]{1,0:T(8,128)(2,1)S(1)}, bf16[2048,512]{1,0:T(8,128)(2,1)}, u32[]{:S(2)}) copy-start(bf16[2048,512]{1,0:T(8,128)(2,1)} %w_ref.4) | copy-start | bytes 6291460
  2.0 3.5 %collective-permute-start = (bf16[32,512]{1,0:T(8,128)(2,1)S(1)}, bf16[32,512]{1,0:T(8,128)(2,1)S(1)}, u32[]{:S(2)}, u32[]{:S(2)}) collective-permute-start(bf16[32,512]{1,0:T(8,128)(2,1)S(1)} %queries.1), channel_id=1, source_target_pairs={{0,4},{4,0},{1,5},{5,1},{2,6},{6,2},{3,7},{7,3},{8,12},{12,8},{9,1... | collective-permute-start | bytes 98312 | tf_op jit(solution)/shard_map/ppermute | solution.py:366
  5.5 9.6 %collective-permute-start.3 = (bf16[64,512]{1,0:T(8,128)(2,1)S(1)}, bf16[64,512]{1,0:T(8,128)(2,1)S(1)}, u32[]{:S(2)}, u32[]{:S(2)}) collective-permute-start(bf16[64,512]{1,0:T(8,128)(2,1)S(1)} %maximum_select_fusion.after_ref), channel_id=1, source_target_pairs={{0,24},{1,97},{8,0},{9,105},{16,8},{17,113},{24,16},{25,121},{32,5... | collective-permute-start | bytes 196616 | tf_op jit(solution)/shard_map/ppermute | solution.py:383
  8.2 6.9 %collective-permute-start.2 = (bf16[64,512]{1,0:T(8,128)(2,1)S(1)}, bf16[64,512]{1,0:T(8,128)(2,1)S(1)}, u32[]{:S(2)}, u32[]{:S(2)}) collective-permute-start(bf16[64,512]{1,0:T(8,128)(2,1)S(1)} %maximum_select_fusion.after_ref), channel_id=1, source_target_pairs={{0,16},{1,65},{8,24},{9,73},{16,0},{17,81},{24,8},{25,89},{32,48},... | collective-permute-start | bytes 196616 | tf_op jit(solution)/shard_map/ppermute | solution.py:383
  8.7 6.4 %collective-permute-start.1 = (bf16[64,512]{1,0:T(8,128)(2,1)S(1)}, bf16[64,512]{1,0:T(8,128)(2,1)S(1)}, u32[]{:S(2)}, u32[]{:S(2)}) collective-permute-start(bf16[64,512]{1,0:T(8,128)(2,1)S(1)} %maximum_select_fusion.after_ref), channel_id=1, source_target_pairs={{0,8},{1,33},{8,16},{9,41},{16,24},{17,49},{24,0},{25,57},{32,40},... | collective-permute-start | bytes 196616 | tf_op jit(solution)/shard_map/ppermute | solution.py:383
  9.4 3.4 %copy-start = (bf16[2048,2048]{1,0:T(8,128)(2,1)S(1)}, bf16[2048,2048]{1,0:T(8,128)(2,1)}, u32[]{:S(2)}) copy-start(bf16[2048,2048]{1,0:T(8,128)(2,1)} %context_ref.5) | copy-start | bytes 25165828
  12.7 7.7 %copy-start.8 = (bf16[2048,512]{1,0:T(8,128)(2,1)S(1)}, bf16[2048,512]{1,0:T(8,128)(2,1)}, u32[]{:S(2)}) copy-start(bf16[2048,512]{1,0:T(8,128)(2,1)} %w_ref.5) | copy-start | bytes 6291460
  15.2 12.0 %collective-permute-start.4 = (bf16[256,512]{1,0:T(8,128)(2,1)S(1)}, bf16[256,512]{1,0:T(8,128)(2,1)S(1)}, u32[]{:S(2)}, u32[]{:S(2)}) collective-permute-start(bf16[256,512]{1,0:T(8,128)(2,1)S(1)} %pad_maximum_fusion.1.after_ref.rest_0_), channel_id=1, source_target_pairs={{0,64},{1,17},{8,72},{9,25},{16,80},{17,1},{24,88},{25,9},{32,96},... | collective-permute-start | bytes 786440 | tf_op jit(solution)/shard_map/ppermute | solution.py:383
  18.9 8.3 %collective-permute-start.5 = (bf16[256,512]{1,0:T(8,128)(2,1)S(1)}, bf16[256,512]{1,0:T(8,128)(2,1)S(1)}, u32[]{:S(2)}, u32[]{:S(2)}) collective-permute-start(bf16[256,512]{1,0:T(8,128)(2,1)S(1)} %pad_maximum_fusion.1.after_ref.rest_0_), channel_id=1, source_target_pairs={{0,96},{1,25},{8,104},{9,1},{16,112},{17,9},{24,120},{25,17},{32,0... | collective-permute-start | bytes 786440 | tf_op jit(solution)/shard_map/ppermute | solution.py:383
  19.4 17.2 %collective-permute-start.8 = (bf16[256,512]{1,0:T(8,128)(2,1)S(1)}, bf16[256,512]{1,0:T(8,128)(2,1)S(1)}, u32[]{:S(2)}, u32[]{:S(2)}) collective-permute-start(bf16[256,512]{1,0:T(8,128)(2,1)S(1)} %pad_maximum_fusion.1.after_ref.rest_0_), channel_id=1, source_target_pairs={{0,32},{1,9},{8,40},{9,17},{16,48},{17,25},{24,56},{25,1},{32,64},... | collective-permute-start | bytes 786440 | tf_op jit(solution)/shard_map/ppermute | solution.py:383
  34.2 11.6 %collective-permute-start.6 = (bf16[256,640]{1,0:T(8,128)(2,1)S(1)}, bf16[256,640]{1,0:T(8,128)(2,1)S(1)}, u32[]{:S(2)}, u32[]{:S(2)}) collective-permute-start(bf16[256,640]{1,0:T(8,128)(2,1)S(1)} %get-tuple-element.16), channel_id=1, source_target_pairs={{0,64},{1,17},{8,72},{9,25},{16,80},{17,1},{24,88},{25,9},{32,96},... | collective-permute-start | bytes 983048 | tf_op jit(solution)/shard_map/ppermute | solution.py:383
  35.4 10.5 %collective-permute-start.7 = (bf16[256,640]{1,0:T(8,128)(2,1)S(1)}, bf16[256,640]{1,0:T(8,128)(2,1)S(1)}, u32[]{:S(2)}, u32[]{:S(2)}) collective-permute-start(bf16[256,640]{1,0:T(8,128)(2,1)S(1)} %get-tuple-element.17), channel_id=1, source_target_pairs={{0,32},{1,9},{8,40},{9,17},{16,48},{17,25},{24,56},{25,1},{32,64},... | collective-permute-start | bytes 983048 | tf_op jit(solution)/shard_map/ppermute | solution.py:383
  40.3 6.3 %collective-permute-start.9 = (bf16[256,640]{1,0:T(8,128)(2,1)S(1)}, bf16[256,640]{1,0:T(8,128)(2,1)S(1)}, u32[]{:S(2)}, u32[]{:S(2)}) collective-permute-start(bf16[256,640]{1,0:T(8,128)(2,1)S(1)} %cross.4), channel_id=1, source_target_pairs={{0,96},{1,25},{8,104},{9,1},{16,112},{17,9},{24,120},{25,17},{32,0... | collective-permute-start | bytes 983048 | tf_op jit(solution)/shard_map/ppermute | solution.py:383
  41.9 29.4 %copy-start.5 = (bf16[2048,512]{1,0:T(8,128)(2,1)S(1)}, bf16[2048,512]{1,0:T(8,128)(2,1)}, u32[]{:S(2)}) copy-start(bf16[2048,512]{1,0:T(8,128)(2,1)} %wk_ref.1) | copy-start | bytes 6291460
  41.9 29.4 %copy-start.6 = (bf16[2048,512]{1,0:T(8,128)(2,1)S(1)}, bf16[2048,512]{1,0:T(8,128)(2,1)}, u32[]{:S(2)}) copy-start(bf16[2048,512]{1,0:T(8,128)(2,1)} %wv_ref.1) | copy-start | bytes 6291460
  45.8 12.3 %copy-start.2 = (bf16[512,2048]{1,0:T(8,128)(2,1)S(1)}, bf16[512,2048]{1,0:T(8,128)(2,1)}, u32[]{:S(2)}) copy-start(bf16[512,2048]{1,0:T(8,128)(2,1)} %wo_ref.2) | copy-start | bytes 6291460
  47.6 23.8 %copy-start.4 = (bf16[2048,512]{1,0:T(8,128)(2,1)S(1)}, bf16[2048,512]{1,0:T(8,128)(2,1)}, u32[]{:S(2)}) copy-start(bf16[2048,512]{1,0:T(8,128)(2,1)} %wq_ref.3) | copy-start | bytes 6291460
  47.6 23.7 %copy-start.7 = (bf16[32,2048]{1,0:T(8,128)(2,1)S(1)}, bf16[32,2048]{1,0:T(8,128)(2,1)}, u32[]{:S(2)}) copy-start(bf16[32,2048]{1,0:T(8,128)(2,1)} %latent_ref.3) | copy-start | bytes 393220
  58.9 6.0 %collective-permute-start.10 = (bf16[32,2048]{1,0:T(8,128)(2,1)S(1)}, bf16[32,2048]{1,0:T(8,128)(2,1)S(1)}, u32[]{:S(2)}, u32[]{:S(2)}) collective-permute-start(bf16[32,2048]{1,0:T(8,128)(2,1)S(1)} %cross_output.1), channel_id=1, source_target_pairs={{0,1},{1,0},{2,3},{3,2},{4,5},{5,4},{6,7},{7,6},{8,9},{9,8},{10,11... | collective-permute-start | bytes 393224 | tf_op jit(solution)/shard_map/ppermute | solution.py:366
  65.0 6.3 %collective-permute-start.11 = (bf16[32,2048]{1,0:T(8,128)(2,1)S(1)}, bf16[32,2048]{1,0:T(8,128)(2,1)S(1)}, u32[]{:S(2)}, u32[]{:S(2)}) collective-permute-start(bf16[32,2048]{1,0:T(8,128)(2,1)S(1)} %add_convert_fusion.2.one_ref), channel_id=1, source_target_pairs={{0,2},{2,0},{1,3},{3,1},{4,6},{6,4},{5,7},{7,5},{8,10},{10,8},{9,1... | collective-permute-start | bytes 393224 | tf_op jit(solution)/shard_map/ppermute | solution.py:366
  73.2 23.2 %copy-start.3 = (bf16[512,2048]{1,0:T(8,128)(2,1)S(1)}, bf16[512,2048]{1,0:T(8,128)(2,1)}, u32[]{:S(2)}) copy-start(bf16[512,2048]{1,0:T(8,128)(2,1)} %wo_ref.3) | copy-start | bytes 6291460
  73.2 2.7 %collective-permute-start.14 = (bf16[32,384]{1,0:T(8,128)(2,1)S(1)}, bf16[32,384]{1,0:T(8,128)(2,1)S(1)}, u32[]{:S(2)}, u32[]{:S(2)}) collective-permute-start(bf16[32,384]{1,0:T(8,128)(2,1)S(1)} %get-tuple-element.22), channel_id=1, source_target_pairs={{0,96},{1,25},{8,104},{9,1},{16,112},{17,9},{24,120},{25,17},{32,0... | collective-permute-start | bytes 73736 | tf_op jit(solution)/shard_map/ppermute | solution.py:383
  74.1 4.2 %collective-permute-start.13 = (bf16[32,384]{1,0:T(8,128)(2,1)S(1)}, bf16[32,384]{1,0:T(8,128)(2,1)S(1)}, u32[]{:S(2)}, u32[]{:S(2)}) collective-permute-start(bf16[32,384]{1,0:T(8,128)(2,1)S(1)} %get-tuple-element.21), channel_id=1, source_target_pairs={{0,64},{1,17},{8,72},{9,25},{16,80},{17,1},{24,88},{25,9},{32,96},... | collective-permute-start | bytes 73736 | tf_op jit(solution)/shard_map/ppermute | solution.py:383
  75.3 3.9 %collective-permute-start.12 = (bf16[32,384]{1,0:T(8,128)(2,1)S(1)}, bf16[32,384]{1,0:T(8,128)(2,1)S(1)}, u32[]{:S(2)}, u32[]{:S(2)}) collective-permute-start(bf16[32,384]{1,0:T(8,128)(2,1)S(1)} %get-tuple-element.20), channel_id=1, source_target_pairs={{0,32},{1,9},{8,40},{9,17},{16,48},{17,25},{24,56},{25,1},{32,64},... | collective-permute-start | bytes 73736 | tf_op jit(solution)/shard_map/ppermute | solution.py:383
  91.3 2.6 %collective-permute-start.15 = (bf16[32,128]{1,0:T(8,128)(2,1)S(1)}, bf16[32,128]{1,0:T(8,128)(2,1)S(1)}, u32[]{:S(2)}, u32[]{:S(2)}) collective-permute-start(bf16[32,128]{1,0:T(8,128)(2,1)S(1)} %get-tuple-element.24), channel_id=1, source_target_pairs={{0,96},{1,25},{8,104},{9,1},{16,112},{17,9},{24,120},{25,17},{32,0... | collective-permute-start | bytes 24584 | tf_op jit(solution)/shard_map/ppermute | solution.py:383
  91.7 4.0 %collective-permute-start.16 = (bf16[32,128]{1,0:T(8,128)(2,1)S(1)}, bf16[32,128]{1,0:T(8,128)(2,1)S(1)}, u32[]{:S(2)}, u32[]{:S(2)}) collective-permute-start(bf16[32,128]{1,0:T(8,128)(2,1)S(1)} %get-tuple-element.25), channel_id=1, source_target_pairs={{0,64},{1,17},{8,72},{9,25},{16,80},{17,1},{24,88},{25,9},{32,96},... | collective-permute-start | bytes 24584 | tf_op jit(solution)/shard_map/ppermute | solution.py:383
  92.7 3.7 %collective-permute-start.17 = (bf16[32,128]{1,0:T(8,128)(2,1)S(1)}, bf16[32,128]{1,0:T(8,128)(2,1)S(1)}, u32[]{:S(2)}, u32[]{:S(2)}) collective-permute-start(bf16[32,128]{1,0:T(8,128)(2,1)S(1)} %get-tuple-element.26), channel_id=1, source_target_pairs={{0,32},{1,9},{8,40},{9,17},{16,48},{17,25},{24,56},{25,1},{32,64},... | collective-permute-start | bytes 24584 | tf_op jit(solution)/shard_map/ppermute | solution.py:383
  97.4 6.5 %collective-permute-start.18 = (bf16[32,2048]{1,0:T(8,128)(2,1)S(1)}, bf16[32,2048]{1,0:T(8,128)(2,1)S(1)}, u32[]{:S(2)}, u32[]{:S(2)}) collective-permute-start(bf16[32,2048]{1,0:T(8,128)(2,1)S(1)} %self_output.1), channel_id=1, source_target_pairs={{0,1},{1,0},{2,3},{3,2},{4,5},{5,4},{6,7},{7,6},{8,9},{9,8},{10,11... | collective-permute-start | bytes 393224 | tf_op jit(solution)/shard_map/ppermute | solution.py:366
  103.9 6.3 %collective-permute-start.19 = (bf16[32,2048]{1,0:T(8,128)(2,1)S(1)}, bf16[32,2048]{1,0:T(8,128)(2,1)S(1)}, u32[]{:S(2)}, u32[]{:S(2)}) collective-permute-start(bf16[32,2048]{1,0:T(8,128)(2,1)S(1)} %add_convert_fusion.1), channel_id=1, source_target_pairs={{0,2},{2,0},{1,3},{3,1},{4,6},{6,4},{5,7},{7,5},{8,10},{10,8},{9,1... | collective-permute-start | bytes 393224 | tf_op jit(solution)/shard_map/ppermute | solution.py:366

commit v2 on v1

--- a/solution.py
+++ b/solution.py
@@ -103,7 +103,7 @@
     width = context.shape[1]
     cols = weight.shape[1]
     return pl.pallas_call(
-        functools.partial(context_kernel, first, min(512, rows)),
+        functools.partial(context_kernel, first, 512 if rows % 512 == 0 else 256),
         out_shape=shape_of((rows, cols)),
         in_specs=[VMEM, VMEM, pl.BlockSpec(memory_space=pl.ANY)],
         out_specs=VMEM,
@@ -111,6 +111,40 @@
         cost_estimate=cost(2 * rows * width * cols, 2 * (rows * width + width * cols)),
         name=name,
     )(context, weight, after)
+
+
+def first_kernel(context_ref, w_ref, after_ref, out_ref, held, sems):
+    pieces, step = held.shape[:2]
+    copies = [
+        pltpu.make_async_copy(context_ref.at[pl.ds(i * step, step)], held.at[i], sems.at[i])
+        for i in range(pieces)
+    ]
+    for copy in copies:
+        copy.start()
+    for i, copy in enumerate(copies):
+        copy.wait()
+        tile = held[i]
+        product = dot(tile, w_ref[...]) * inv_rms(tile.astype(F32))
+        out_ref[pl.ds(i * step, step), :] = product.astype(BF16)
+
+
+def first_project(context, weight, after, rows):
+    width = context.shape[1]
+    cols = weight.shape[1]
+    pieces = 4
+    return pl.pallas_call(
+        first_kernel,
+        out_shape=shape_of((rows, cols)),
+        in_specs=[HBM, VMEM, pl.BlockSpec(memory_space=pl.ANY)],
+        out_specs=VMEM,
+        scratch_shapes=[
+            pltpu.VMEM((pieces, rows // pieces, width), BF16),
+            pltpu.SemaphoreType.DMA((pieces,)),
+        ],
+        compiler_params=params(20),
+        cost_estimate=cost(2 * rows * width * cols, 2 * (rows * width + width * cols)),
+        name="first_keys",
+    )(pltpu.with_memory_space_constraint(context, pltpu.HBM), weight, after)
 
 
 def packed_totals(totals):
@@ -430,16 +464,17 @@
     pair = jnp.where(
         y_lo == 0, jnp.concatenate([own, other]), jnp.concatenate([other, own])
     )
-    half = context.shape[0] // 2
-    keys = [project_context(context, wk_cross, pair, "keys", 0, half)]
+    whole = context.shape[0]
+    part = whole // 2
+    keys = [first_project(context, wk_cross, pair, part)]
     came = {offset: turned(pair, "b", offset) for offset in (2, 1, 3)}
     ring = [pair] + [came[offset] for offset in (1, 2, 3)]
     pieces = [
         lax.dynamic_index_in_dim(jnp.stack(ring), (b - place) & 3, 0, False) for place in range(4)
     ]
     mine = jnp.concatenate(pieces)
-    keys.append(project_context(context, wk_cross, mine, "keys", half, half))
-    values = project_context(context, wv_cross, mine, "values", 0, 2 * half)
+    keys.append(project_context(context, wk_cross, mine, "keys", part, whole - part))
+    values = project_context(context, wv_cross, mine, "values", 0, whole)
     blocks = {0: mine}
     for offset in (2, 3, 1):
         blocks[(4 - offset) % 4] = turned(mine, "a", offset)

time: 111 us -> 110 us (level)
  local copies, waits for them, and re-layouts: 3.93 us -> 0.56 us
  Pallas kernels: 31.3 us -> 33.2 us
    unnamed x20, local copies, waits for them, and re-layouts: 3.43 us -> 0.05 us
    pallas_call x3, Pallas kernels: 9.18 us -> 11.1 us  [the longest x2 6.85 us: project_context(): pl.pallas_call(functools.partial(context_kernel, first, 512 if rows % 512...]
  transfers between devices with their start and end apart: 20 -> 20, of which waited for: 12 -> 12; matrix products, arithmetic and copies ran while one was open for 0% -> 0% of each run, Pallas kernels for 21% -> 23%
where the time goes in v2:
time: 110 us
  starting transfers between devices  34.9 us (32%)
  Pallas kernels  33.2 us (30%)
  blocking collectives  22.2 us (20%)
  waiting for transfers between devices  18.1 us (16%)
    all_to_all x2, blocking collectives, exchanged(): return lax.all_to_all(tensor, WHOLE, 0, 0, axis_index_groups=groups)  22.2 us
    ppermute x5, starting transfers between devices, moved(): lax.ppermute(tensor, axis, [(i, (i + offset) % size) for i in range(size)])  18.3 us
    ppermute x15, starting transfers between devices, turned(): return lax.ppermute(tensor, PLANE, pairs)  16.6 us
    pallas_call x3, Pallas kernels, cross_attend(): pl.pallas_call(functools.partial(cross_kernel, offsets), out_shape=[shape...  14.5 us
    ppermute x5, waiting for transfers between devices, moved(): lax.ppermute(tensor, axis, [(i, (i + offset) % size) for i in range(size)])  9.91 us
    ppermute x15, waiting for transfers between devices, turned(): return lax.ppermute(tensor, PLANE, pairs)  8.16 us
    pallas_call x2, Pallas kernels, project_context(): pl.pallas_call(functools.partial(context_kernel, first, 512 if rows % 512...  6.85 us
    pallas_call x1, Pallas kernels, first_project(): pl.pallas_call(first_kernel, out_shape=shape_of((rows, cols)), in_specs=[...  4.24 us
  transfers between devices with their start and end apart: 20, of which 12 were waited for; matrix products, arithmetic and copies ran while one was open for 0% of the time, Pallas kernels for 23%

profile of v2, /device:TPU:1, one launch (start us, length us, event | category | flops | bytes accessed | tf_op | source)
XLA Modules:
  0.0 110.1 jit_solution(7163579357976057008)
XLA Ops:
  0.0 2.0 %queries.1 = bf16[32,512]{1,0:T(8,128)(2,1)S(1)} custom-call(bf16[32,2048]{1,0:T(8,128)(2,1)} %latent_ref.3, bf16[2048,512]{1,0:T(8,128)(2,1)} %wq_ref.2), custom_call_target="tpu_custom_call" | custom-call | flops 67108864 | bytes 2097152 | tf_op jit(solution)/shard_map/queries/pallas_call | solution.py:72
  2.0 2.2 %collective-permute-start = (bf16[32,512]{1,0:T(8,128)(2,1)S(1)}, bf16[32,512]{1,0:T(8,128)(2,1)S(1)}, u32[]{:S(2)}, u32[]{:S(2)}) collective-permute-start(bf16[32,512]{1,0:T(8,128)(2,1)S(1)} %queries.1), channel_id=1, source_target_pairs={{0,4},{4,0},{1,5},{5,1},{2,6},{6,2},{3,7},{7,3},{8,12},{12,8},{9,1... | collective-permute-start | bytes 98312 | tf_op jit(solution)/shard_map/ppermute | solution.py:400
  4.4 0.1 stack.55.ids_ref
  4.4 1.0 collective-permute-done
  5.5 2.7 %collective-permute-start.3 = (bf16[64,512]{1,0:T(8,128)(2,1)S(1)}, bf16[64,512]{1,0:T(8,128)(2,1)S(1)}, u32[]{:S(2)}, u32[]{:S(2)}) collective-permute-start(bf16[64,512]{1,0:T(8,128)(2,1)S(1)} %maximum_select_fusion.after_ref), channel_id=1, source_target_pairs={{0,24},{1,97},{8,0},{9,105},{16,8},{17,113},{24,16},{25,121},{32,5... | collective-permute-start | bytes 196616 | tf_op jit(solution)/shard_map/ppermute | solution.py:417
  8.2 0.5 collective-permute-start.2
  8.8 0.6 collective-permute-start.1
  9.4 4.2 %first_keys.1.k_ref = bf16[1024,512]{1,0:T(8,128)(2,1)S(1)} custom-call(bf16[2048,2048]{1,0:T(8,128)(2,1)} %context_ref.5, bf16[2048,512]{1,0:T(8,128)(2,1)S(1)} %copy-done.1, bf16[64,512]{1,0:T(8,128)(2,1)S(1)} %maximum_select_fusion.after_ref), custom_call_target="tpu_custom_call" | custom-call | flops 2147483648 | bytes 6291456 | tf_op jit(solution)/shard_map/first_keys/pallas_call | solution.py:135
  13.8 3.7 %collective-permute-start.4 = (bf16[256,512]{1,0:T(8,128)(2,1)S(1)}, bf16[256,512]{1,0:T(8,128)(2,1)S(1)}, u32[]{:S(2)}, u32[]{:S(2)}) collective-permute-start(bf16[256,512]{1,0:T(8,128)(2,1)S(1)} %pad_maximum_fusion.1.after_ref.rest_0_), channel_id=1, source_target_pairs={{0,64},{1,17},{8,72},{9,25},{16,80},{17,1},{24,88},{25,9},{32,96},... | collective-permute-start | bytes 786440 | tf_op jit(solution)/shard_map/ppermute | solution.py:417
  17.5 0.5 collective-permute-start.5
  17.9 1.0 collective-permute-start.8
  18.9 4.5 %values.1.v_ref = bf16[2048,512]{1,0:T(8,128)(2,1)S(1)} custom-call(bf16[2048,2048]{1,0:T(8,128)(2,1)S(1)} %copy-done, bf16[2048,512]{1,0:T(8,128)(2,1)S(1)} %copy-done.8, bf16[256,512]{1,0:T(8,128)(2,1)S(1)} %pad_maximum_fusion.1.after_ref.rest_0_), custom_call_target="tpu_custom_call" | custom-call | flops 4294967296 | bytes 10485760 | tf_op jit(solution)/shard_map/values/pallas_call | solution.py:105
  23.5 2.3 %keys.1.more_ref = bf16[1024,512]{1,0:T(8,128)(2,1)S(1)} custom-call(bf16[2048,2048]{1,0:T(8,128)(2,1)S(1)} %copy-done, bf16[2048,512]{1,0:T(8,128)(2,1)S(1)} %copy-done.1, bf16[256,512]{1,0:T(8,128)(2,1)S(1)} %pad_maximum_fusion.1.after_ref.rest_0_), custom_call_target="tpu_custom_call" | custom-call | flops 2147483648 | bytes 6291456 | tf_op jit(solution)/shard_map/keys/pallas_call | solution.py:105
  25.8 0.2 broadcast_in_dim.4.cut_ref
  26.0 6.8 %cross.3 = (bf16[256,640]{1,0:T(8,128)(2,1)S(1)}, bf16[256,640]{1,0:T(8,128)(2,1)S(1)}) custom-call(s32[6]{0:T(128)S(1)} %stack.55.ids_ref, s32[1024]{0:T(1024)S(1)} %broadcast_select_fusion.cutoff_ref, s32[1024,128]{1,0:T(8,128)S(1)} %broadcast_in_dim.4.cut_ref, bf16[1024,512]{1,0:T(8,128)(2,1)S(1)} %first_keys.1.k_ref, ...), custom_call_target="tpu_custom_call" | custom-call | flops 4294967296 | bytes 4194304 | tf_op jit(solution)/shard_map/cross/pallas_call | solution.py:243
  32.8 1.2 %collective-permute-start.6 = (bf16[256,640]{1,0:T(8,128)(2,1)S(1)}, bf16[256,640]{1,0:T(8,128)(2,1)S(1)}, u32[]{:S(2)}, u32[]{:S(2)}) collective-permute-start(bf16[256,640]{1,0:T(8,128)(2,1)S(1)} %get-tuple-element.16), channel_id=1, source_target_pairs={{0,64},{1,17},{8,72},{9,25},{16,80},{17,1},{24,88},{25,9},{32,96},... | collective-permute-start | bytes 983048 | tf_op jit(solution)/shard_map/ppermute | solution.py:417
  33.9 1.2 %collective-permute-start.7 = (bf16[256,640]{1,0:T(8,128)(2,1)S(1)}, bf16[256,640]{1,0:T(8,128)(2,1)S(1)}, u32[]{:S(2)}, u32[]{:S(2)}) collective-permute-start(bf16[256,640]{1,0:T(8,128)(2,1)S(1)} %get-tuple-element.17), channel_id=1, source_target_pairs={{0,32},{1,9},{8,40},{9,17},{16,48},{17,25},{24,56},{25,1},{32,64},... | collective-permute-start | bytes 983048 | tf_op jit(solution)/shard_map/ppermute | solution.py:417
  35.1 3.7 %cross.4 = bf16[256,640]{1,0:T(8,128)(2,1)S(1)} custom-call(s32[6]{0:T(128)S(1)} %stack.55.ids_ref, s32[1024]{0:T(1024)S(1)} %broadcast_select_fusion.cutoff_ref, s32[1024,128]{1,0:T(8,128)S(1)} %broadcast_in_dim.4.cut_ref, bf16[1024,512]{1,0:T(8,128)(2,1)S(1)} %first_keys.1.k_ref, bf16[1024,512]{1,0:T(8,128)(2,1)S(1)} %keys.1.more_ref, ...), custom_call_target="tpu_custom_call" | custom-call | flops 2147483648 | bytes 4194304 | tf_op jit(solution)/shard_map/cross/pallas_call | solution.py:243
  38.9 1.6 %collective-permute-start.9 = (bf16[256,640]{1,0:T(8,128)(2,1)S(1)}, bf16[256,640]{1,0:T(8,128)(2,1)S(1)}, u32[]{:S(2)}, u32[]{:S(2)}) collective-permute-start(bf16[256,640]{1,0:T(8,128)(2,1)S(1)} %cross.4), channel_id=1, source_target_pairs={{0,96},{1,25},{8,104},{9,1},{16,112},{17,9},{24,120},{25,17},{32,0... | collective-permute-start | bytes 983048 | tf_op jit(solution)/shard_map/ppermute | solution.py:417
  40.4 4.0 %cross.5.d_ref = bf16[256,640]{1,0:T(8,128)(2,1)S(1)} custom-call(s32[6]{0:T(128)S(1)} %stack.55.ids_ref, s32[1024]{0:T(1024)S(1)} %broadcast_select_fusion.cutoff_ref, s32[1024,128]{1,0:T(8,128)S(1)} %broadcast_in_dim.4.cut_ref, bf16[1024,512]{1,0:T(8,128)(2,1)S(1)} %first_keys.1.k_ref, bf16[1024,512]{1,0:T(8,128)(2,1)S(1)} %keys.1.more_ref, ...), custom_call_target="tpu_custom_call" | custom-call | flops 2147483648 | bytes 4194304 | tf_op jit(solution)/shard_map/cross/pallas_call | solution.py:243
  44.4 0.7 collective-permute-done.9.c_ref
  45.1 1.0 blend.1
  46.2 10.7 %all_to_all.10.parts_ref = bf16[8,32,640]{2,1,0:T(8,128)(2,1)S(1)} all-to-all(bf16[8,32,640]{2,1,0:T(8,128)(2,1)S(1)} %bitcast.21), channel_id=1, replica_groups={{0,4,8,12,16,20,24,28},{1,5,33,37,65,69,97,101},{32,36,40,44,48,52,56,6..., dimensions={0} | all-to-all | bytes 655360 | tf_op jit(solution)/shard_map/all_to_all | solution.py:427
  56.9 0.7 cross_output.1
  57.7 4.9 %collective-permute-start.10 = (bf16[32,2048]{1,0:T(8,128)(2,1)S(1)}, bf16[32,2048]{1,0:T(8,128)(2,1)S(1)}, u32[]{:S(2)}, u32[]{:S(2)}) collective-permute-start(bf16[32,2048]{1,0:T(8,128)(2,1)S(1)} %cross_output.1), channel_id=1, source_target_pairs={{0,1},{1,0},{2,3},{3,2},{4,5},{5,4},{6,7},{7,6},{8,9},{9,8},{10,11... | collective-permute-start | bytes 393224 | tf_op jit(solution)/shard_map/ppermute | solution.py:400
  62.5 1.0 collective-permute-done.10
  63.5 2.7 %collective-permute-start.11 = (bf16[32,2048]{1,0:T(8,128)(2,1)S(1)}, bf16[32,2048]{1,0:T(8,128)(2,1)S(1)}, u32[]{:S(2)}, u32[]{:S(2)}) collective-permute-start(bf16[32,2048]{1,0:T(8,128)(2,1)S(1)} %add_convert_fusion.2.one_ref), channel_id=1, source_target_pairs={{0,2},{2,0},{1,3},{3,1},{4,6},{6,4},{5,7},{7,5},{8,10},{10,8},{9,1... | collective-permute-start | bytes 393224 | tf_op jit(solution)/shard_map/ppermute | solution.py:400
  66.3 3.6 %collective-permute-done.11.two_ref = bf16[32,2048]{1,0:T(8,128)(2,1)S(1)} collective-permute-done((bf16[32,2048]{1,0:T(8,128)(2,1)S(1)}, bf16[32,2048]{1,0:T(8,128)(2,1)S(1)}, u32[]{:S(2)}, u32[]{:S(2)}) %collective-permute-start.11) | collective-permute-done | bytes 131104 | tf_op jit(solution)/shard_map/ppermute | solution.py:400
  69.9 1.8 %self_project.1 = (f32[32,2048]{1,0:T(8,128)S(1)}, bf16[32,384]{1,0:T(8,128)(2,1)S(1)}, bf16[32,384]{1,0:T(8,128)(2,1)S(1)}, bf16[32,384]{1,0:T(8,128)(2,1)S(1)}, bf16[32,384]{1,0:T(8,128)(2,1)S(1)}) custom-call(s32[6]{0:T(128)S(1)} %stack.55.ids_ref, bf16[32,2048]{1,0:T(8,128)(2,1)S(1)} %copy-done.7, bf16[32,2048]{1,0:T(8,128)(2,1)S(1)} %add_convert_fusion.2.one_ref, ...), custom_call_target="tpu_custom_call" | custom-call | tf_op jit(solution)/shard_map/self_project/pallas_call | solution.py:331
  71.7 1.0 collective-permute-start.14
  72.7 1.2 %collective-permute-start.13 = (bf16[32,384]{1,0:T(8,128)(2,1)S(1)}, bf16[32,384]{1,0:T(8,128)(2,1)S(1)}, u32[]{:S(2)}, u32[]{:S(2)}) collective-permute-start(bf16[32,384]{1,0:T(8,128)(2,1)S(1)} %get-tuple-element.21), channel_id=1, source_target_pairs={{0,64},{1,17},{8,72},{9,25},{16,80},{17,1},{24,88},{25,9},{32,96},... | collective-permute-start | bytes 73736 | tf_op jit(solution)/shard_map/ppermute | solution.py:417
  73.9 0.6 collective-permute-done.14.d_ref
  74.5 2.4 %collective-permute-done.13.c_ref = bf16[32,384]{1,0:T(8,128)(2,1)S(1)} collective-permute-done((bf16[32,384]{1,0:T(8,128)(2,1)S(1)}, bf16[32,384]{1,0:T(8,128)(2,1)S(1)}, u32[]{:S(2)}, u32[]{:S(2)}) %collective-permute-start.13) | collective-permute-done | bytes 24608 | tf_op jit(solution)/shard_map/ppermute | solution.py:417
  76.9 0.9 collective-permute-done.12.b_ref
  77.8 11.5 %all_to_all.11.kv_ref = bf16[8,128,256]{2,1,0:T(8,128)(2,1)S(1)} all-to-all(bf16[8,128,256]{2,1,0:T(8,128)(2,1)S(1)} %broadcast_in_dim.5), channel_id=1, replica_groups={{0,4,8,12,16,20,24,28},{1,5,33,37,65,69,97,101},{32,36,40,44,48,52,56,6..., dimensions={0} | all-to-all | bytes 1048576 | tf_op jit(solution)/shard_map/all_to_all | solution.py:427
  89.3 1.1 %self_attend.1 = (bf16[32,128]{1,0:T(8,128)(2,1)S(1)}, bf16[32,128]{1,0:T(8,128)(2,1)S(1)}, bf16[32,128]{1,0:T(8,128)(2,1)S(1)}, bf16[32,128]{1,0:T(8,128)(2,1)S(1)}) custom-call(s32[6]{0:T(128)S(1)} %stack.55.ids_ref, bf16[32,384]{1,0:T(8,128)(2,1)S(1)} %get-tuple-element.19.a_ref, bf16[32,384]{1,0:T(8,128)(2,1)S(1)} %collective-permute-done.12.b_ref, ...), custom_call_target="tpu_custom_call" | custom-call | tf_op jit(solution)/shard_map/self_attend/pallas_call | solution.py:369
  90.4 0.7 collective-permute-start.15
  91.1 0.7 collective-permute-start.16
  91.8 0.1 collective-permute-start.17
  92.0 1.0 collective-permute-done.15.b_ref
  93.0 2.1 %collective-permute-done.16.c_ref = bf16[32,128]{1,0:T(8,128)(2,1)S(1)} collective-permute-done((bf16[32,128]{1,0:T(8,128)(2,1)S(1)}, bf16[32,128]{1,0:T(8,128)(2,1)S(1)}, u32[]{:S(2)}, u32[]{:S(2)}) %collective-permute-start.16) | collective-permute-done | bytes 8224 | tf_op jit(solution)/shard_map/ppermute | solution.py:417
  95.1 0.4 collective-permute-done.17.d_ref
  95.5 1.0 self_output.1
  96.5 5.5 %collective-permute-start.18 = (bf16[32,2048]{1,0:T(8,128)(2,1)S(1)}, bf16[32,2048]{1,0:T(8,128)(2,1)S(1)}, u32[]{:S(2)}, u32[]{:S(2)}) collective-permute-start(bf16[32,2048]{1,0:T(8,128)(2,1)S(1)} %self_output.1), channel_id=1, source_target_pairs={{0,1},{1,0},{2,3},{3,2},{4,5},{5,4},{6,7},{7,6},{8,9},{9,8},{10,11... | collective-permute-start | bytes 393224 | tf_op jit(solution)/shard_map/ppermute | solution.py:400
  102.0 1.0 collective-permute-done.18
  103.1 3.0 %collective-permute-start.19 = (bf16[32,2048]{1,0:T(8,128)(2,1)S(1)}, bf16[32,2048]{1,0:T(8,128)(2,1)S(1)}, u32[]{:S(2)}, u32[]{:S(2)}) collective-permute-start(bf16[32,2048]{1,0:T(8,128)(2,1)S(1)} %add_convert_fusion.1), channel_id=1, source_target_pairs={{0,2},{2,0},{1,3},{3,1},{4,6},{6,4},{5,7},{7,5},{8,10},{10,8},{9,1... | collective-permute-start | bytes 393224 | tf_op jit(solution)/shard_map/ppermute | solution.py:400
  106.1 3.3 %collective-permute-done.19 = bf16[32,2048]{1,0:T(8,128)(2,1)S(1)} collective-permute-done((bf16[32,2048]{1,0:T(8,128)(2,1)S(1)}, bf16[32,2048]{1,0:T(8,128)(2,1)S(1)}, u32[]{:S(2)}, u32[]{:S(2)}) %collective-permute-start.19) | collective-permute-done | bytes 131104 | tf_op jit(solution)/shard_map/ppermute | solution.py:400
  109.4 0.7 add_convert_fusion
  (46 shorter events, 0.5 us)
Async XLA Ops:
  0.0 4.2 %copy-start.9 = (s32[1024]{0:T(1024)S(1)}, s32[1024]{0:T(1024)}, u32[]{:S(2)}) copy-start(s32[1024]{0:T(1024)} %param.13) | copy-start | bytes 12292
  0.0 9.4 %copy-start.1 = (bf16[2048,512]{1,0:T(8,128)(2,1)S(1)}, bf16[2048,512]{1,0:T(8,128)(2,1)}, u32[]{:S(2)}) copy-start(bf16[2048,512]{1,0:T(8,128)(2,1)} %w_ref.4) | copy-start | bytes 6291460
  2.0 3.5 %collective-permute-start = (bf16[32,512]{1,0:T(8,128)(2,1)S(1)}, bf16[32,512]{1,0:T(8,128)(2,1)S(1)}, u32[]{:S(2)}, u32[]{:S(2)}) collective-permute-start(bf16[32,512]{1,0:T(8,128)(2,1)S(1)} %queries.1), channel_id=1, source_target_pairs={{0,4},{4,0},{1,5},{5,1},{2,6},{6,2},{3,7},{7,3},{8,12},{12,8},{9,1... | collective-permute-start | bytes 98312 | tf_op jit(solution)/shard_map/ppermute | solution.py:400
  5.5 13.4 %copy-start = (bf16[2048,2048]{1,0:T(8,128)(2,1)S(1)}, bf16[2048,2048]{1,0:T(8,128)(2,1)}, u32[]{:S(2)}) copy-start(bf16[2048,2048]{1,0:T(8,128)(2,1)} %context_ref.5) | copy-start | bytes 25165828
  5.5 13.4 %copy-start.8 = (bf16[2048,512]{1,0:T(8,128)(2,1)S(1)}, bf16[2048,512]{1,0:T(8,128)(2,1)}, u32[]{:S(2)}) copy-start(bf16[2048,512]{1,0:T(8,128)(2,1)} %w_ref.5) | copy-start | bytes 6291460
  5.5 8.1 %collective-permute-start.3 = (bf16[64,512]{1,0:T(8,128)(2,1)S(1)}, bf16[64,512]{1,0:T(8,128)(2,1)S(1)}, u32[]{:S(2)}, u32[]{:S(2)}) collective-permute-start(bf16[64,512]{1,0:T(8,128)(2,1)S(1)} %maximum_select_fusion.after_ref), channel_id=1, source_target_pairs={{0,24},{1,97},{8,0},{9,105},{16,8},{17,113},{24,16},{25,121},{32,5... | collective-permute-start | bytes 196616 | tf_op jit(solution)/shard_map/ppermute | solution.py:417
  8.2 5.4 %collective-permute-start.2 = (bf16[64,512]{1,0:T(8,128)(2,1)S(1)}, bf16[64,512]{1,0:T(8,128)(2,1)S(1)}, u32[]{:S(2)}, u32[]{:S(2)}) collective-permute-start(bf16[64,512]{1,0:T(8,128)(2,1)S(1)} %maximum_select_fusion.after_ref), channel_id=1, source_target_pairs={{0,16},{1,65},{8,24},{9,73},{16,0},{17,81},{24,8},{25,89},{32,48},... | collective-permute-start | bytes 196616 | tf_op jit(solution)/shard_map/ppermute | solution.py:417
  8.8 4.9 %collective-permute-start.1 = (bf16[64,512]{1,0:T(8,128)(2,1)S(1)}, bf16[64,512]{1,0:T(8,128)(2,1)S(1)}, u32[]{:S(2)}, u32[]{:S(2)}) collective-permute-start(bf16[64,512]{1,0:T(8,128)(2,1)S(1)} %maximum_select_fusion.after_ref), channel_id=1, source_target_pairs={{0,8},{1,33},{8,16},{9,41},{16,24},{17,49},{24,0},{25,57},{32,40},... | collective-permute-start | bytes 196616 | tf_op jit(solution)/shard_map/ppermute | solution.py:417
  13.8 12.0 %collective-permute-start.4 = (bf16[256,512]{1,0:T(8,128)(2,1)S(1)}, bf16[256,512]{1,0:T(8,128)(2,1)S(1)}, u32[]{:S(2)}, u32[]{:S(2)}) collective-permute-start(bf16[256,512]{1,0:T(8,128)(2,1)S(1)} %pad_maximum_fusion.1.after_ref.rest_0_), channel_id=1, source_target_pairs={{0,64},{1,17},{8,72},{9,25},{16,80},{17,1},{24,88},{25,9},{32,96},... | collective-permute-start | bytes 786440 | tf_op jit(solution)/shard_map/ppermute | solution.py:417
  17.5 8.3 %collective-permute-start.5 = (bf16[256,512]{1,0:T(8,128)(2,1)S(1)}, bf16[256,512]{1,0:T(8,128)(2,1)S(1)}, u32[]{:S(2)}, u32[]{:S(2)}) collective-permute-start(bf16[256,512]{1,0:T(8,128)(2,1)S(1)} %pad_maximum_fusion.1.after_ref.rest_0_), channel_id=1, source_target_pairs={{0,96},{1,25},{8,104},{9,1},{16,112},{17,9},{24,120},{25,17},{32,0... | collective-permute-start | bytes 786440 | tf_op jit(solution)/shard_map/ppermute | solution.py:417
  17.9 17.2 %collective-permute-start.8 = (bf16[256,512]{1,0:T(8,128)(2,1)S(1)}, bf16[256,512]{1,0:T(8,128)(2,1)S(1)}, u32[]{:S(2)}, u32[]{:S(2)}) collective-permute-start(bf16[256,512]{1,0:T(8,128)(2,1)S(1)} %pad_maximum_fusion.1.after_ref.rest_0_), channel_id=1, source_target_pairs={{0,32},{1,9},{8,40},{9,17},{16,48},{17,25},{24,56},{25,1},{32,64},... | collective-permute-start | bytes 786440 | tf_op jit(solution)/shard_map/ppermute | solution.py:417
  32.8 11.6 %collective-permute-start.6 = (bf16[256,640]{1,0:T(8,128)(2,1)S(1)}, bf16[256,640]{1,0:T(8,128)(2,1)S(1)}, u32[]{:S(2)}, u32[]{:S(2)}) collective-permute-start(bf16[256,640]{1,0:T(8,128)(2,1)S(1)} %get-tuple-element.16), channel_id=1, source_target_pairs={{0,64},{1,17},{8,72},{9,25},{16,80},{17,1},{24,88},{25,9},{32,96},... | collective-permute-start | bytes 983048 | tf_op jit(solution)/shard_map/ppermute | solution.py:417
  33.9 10.5 %collective-permute-start.7 = (bf16[256,640]{1,0:T(8,128)(2,1)S(1)}, bf16[256,640]{1,0:T(8,128)(2,1)S(1)}, u32[]{:S(2)}, u32[]{:S(2)}) collective-permute-start(bf16[256,640]{1,0:T(8,128)(2,1)S(1)} %get-tuple-element.17), channel_id=1, source_target_pairs={{0,32},{1,9},{8,40},{9,17},{16,48},{17,25},{24,56},{25,1},{32,64},... | collective-permute-start | bytes 983048 | tf_op jit(solution)/shard_map/ppermute | solution.py:417
  38.9 6.3 %collective-permute-start.9 = (bf16[256,640]{1,0:T(8,128)(2,1)S(1)}, bf16[256,640]{1,0:T(8,128)(2,1)S(1)}, u32[]{:S(2)}, u32[]{:S(2)}) collective-permute-start(bf16[256,640]{1,0:T(8,128)(2,1)S(1)} %cross.4), channel_id=1, source_target_pairs={{0,96},{1,25},{8,104},{9,1},{16,112},{17,9},{24,120},{25,17},{32,0... | collective-permute-start | bytes 983048 | tf_op jit(solution)/shard_map/ppermute | solution.py:417
  40.4 29.4 %copy-start.5 = (bf16[2048,512]{1,0:T(8,128)(2,1)S(1)}, bf16[2048,512]{1,0:T(8,128)(2,1)}, u32[]{:S(2)}) copy-start(bf16[2048,512]{1,0:T(8,128)(2,1)} %wk_ref.1) | copy-start | bytes 6291460
  40.4 29.4 %copy-start.6 = (bf16[2048,512]{1,0:T(8,128)(2,1)S(1)}, bf16[2048,512]{1,0:T(8,128)(2,1)}, u32[]{:S(2)}) copy-start(bf16[2048,512]{1,0:T(8,128)(2,1)} %wv_ref.1) | copy-start | bytes 6291460
  44.4 12.5 %copy-start.2 = (bf16[512,2048]{1,0:T(8,128)(2,1)S(1)}, bf16[512,2048]{1,0:T(8,128)(2,1)}, u32[]{:S(2)}) copy-start(bf16[512,2048]{1,0:T(8,128)(2,1)} %wo_ref.2) | copy-start | bytes 6291460
  46.1 23.7 %copy-start.4 = (bf16[2048,512]{1,0:T(8,128)(2,1)S(1)}, bf16[2048,512]{1,0:T(8,128)(2,1)}, u32[]{:S(2)}) copy-start(bf16[2048,512]{1,0:T(8,128)(2,1)} %wq_ref.3) | copy-start | bytes 6291460
  46.1 23.7 %copy-start.7 = (bf16[32,2048]{1,0:T(8,128)(2,1)S(1)}, bf16[32,2048]{1,0:T(8,128)(2,1)}, u32[]{:S(2)}) copy-start(bf16[32,2048]{1,0:T(8,128)(2,1)} %latent_ref.3) | copy-start | bytes 393220
  57.7 5.9 %collective-permute-start.10 = (bf16[32,2048]{1,0:T(8,128)(2,1)S(1)}, bf16[32,2048]{1,0:T(8,128)(2,1)S(1)}, u32[]{:S(2)}, u32[]{:S(2)}) collective-permute-start(bf16[32,2048]{1,0:T(8,128)(2,1)S(1)} %cross_output.1), channel_id=1, source_target_pairs={{0,1},{1,0},{2,3},{3,2},{4,5},{5,4},{6,7},{7,6},{8,9},{9,8},{10,11... | collective-permute-start | bytes 393224 | tf_op jit(solution)/shard_map/ppermute | solution.py:400
  63.5 6.3 %collective-permute-start.11 = (bf16[32,2048]{1,0:T(8,128)(2,1)S(1)}, bf16[32,2048]{1,0:T(8,128)(2,1)S(1)}, u32[]{:S(2)}, u32[]{:S(2)}) collective-permute-start(bf16[32,2048]{1,0:T(8,128)(2,1)S(1)} %add_convert_fusion.2.one_ref), channel_id=1, source_target_pairs={{0,2},{2,0},{1,3},{3,1},{4,6},{6,4},{5,7},{7,5},{8,10},{10,8},{9,1... | collective-permute-start | bytes 393224 | tf_op jit(solution)/shard_map/ppermute | solution.py:400
  71.7 23.8 %copy-start.3 = (bf16[512,2048]{1,0:T(8,128)(2,1)S(1)}, bf16[512,2048]{1,0:T(8,128)(2,1)}, u32[]{:S(2)}) copy-start(bf16[512,2048]{1,0:T(8,128)(2,1)} %wo_ref.3) | copy-start | bytes 6291460
  71.7 2.7 %collective-permute-start.14 = (bf16[32,384]{1,0:T(8,128)(2,1)S(1)}, bf16[32,384]{1,0:T(8,128)(2,1)S(1)}, u32[]{:S(2)}, u32[]{:S(2)}) collective-permute-start(bf16[32,384]{1,0:T(8,128)(2,1)S(1)} %get-tuple-element.22), channel_id=1, source_target_pairs={{0,96},{1,25},{8,104},{9,1},{16,112},{17,9},{24,120},{25,17},{32,0... | collective-permute-start | bytes 73736 | tf_op jit(solution)/shard_map/ppermute | solution.py:417
  72.7 4.2 %collective-permute-start.13 = (bf16[32,384]{1,0:T(8,128)(2,1)S(1)}, bf16[32,384]{1,0:T(8,128)(2,1)S(1)}, u32[]{:S(2)}, u32[]{:S(2)}) collective-permute-start(bf16[32,384]{1,0:T(8,128)(2,1)S(1)} %get-tuple-element.21), channel_id=1, source_target_pairs={{0,64},{1,17},{8,72},{9,25},{16,80},{17,1},{24,88},{25,9},{32,96},... | collective-permute-start | bytes 73736 | tf_op jit(solution)/shard_map/ppermute | solution.py:417
  73.9 3.9 %collective-permute-start.12 = (bf16[32,384]{1,0:T(8,128)(2,1)S(1)}, bf16[32,384]{1,0:T(8,128)(2,1)S(1)}, u32[]{:S(2)}, u32[]{:S(2)}) collective-permute-start(bf16[32,384]{1,0:T(8,128)(2,1)S(1)} %get-tuple-element.20), channel_id=1, source_target_pairs={{0,32},{1,9},{8,40},{9,17},{16,48},{17,25},{24,56},{25,1},{32,64},... | collective-permute-start | bytes 73736 | tf_op jit(solution)/shard_map/ppermute | solution.py:417
  90.4 2.6 %collective-permute-start.15 = (bf16[32,128]{1,0:T(8,128)(2,1)S(1)}, bf16[32,128]{1,0:T(8,128)(2,1)S(1)}, u32[]{:S(2)}, u32[]{:S(2)}) collective-permute-start(bf16[32,128]{1,0:T(8,128)(2,1)S(1)} %get-tuple-element.24), channel_id=1, source_target_pairs={{0,96},{1,25},{8,104},{9,1},{16,112},{17,9},{24,120},{25,17},{32,0... | collective-permute-start | bytes 24584 | tf_op jit(solution)/shard_map/ppermute | solution.py:417
  91.1 4.0 %collective-permute-start.16 = (bf16[32,128]{1,0:T(8,128)(2,1)S(1)}, bf16[32,128]{1,0:T(8,128)(2,1)S(1)}, u32[]{:S(2)}, u32[]{:S(2)}) collective-permute-start(bf16[32,128]{1,0:T(8,128)(2,1)S(1)} %get-tuple-element.25), channel_id=1, source_target_pairs={{0,64},{1,17},{8,72},{9,25},{16,80},{17,1},{24,88},{25,9},{32,96},... | collective-permute-start | bytes 24584 | tf_op jit(solution)/shard_map/ppermute | solution.py:417
  91.8 3.7 %collective-permute-start.17 = (bf16[32,128]{1,0:T(8,128)(2,1)S(1)}, bf16[32,128]{1,0:T(8,128)(2,1)S(1)}, u32[]{:S(2)}, u32[]{:S(2)}) collective-permute-start(bf16[32,128]{1,0:T(8,128)(2,1)S(1)} %get-tuple-element.26), channel_id=1, source_target_pairs={{0,32},{1,9},{8,40},{9,17},{16,48},{17,25},{24,56},{25,1},{32,64},... | collective-permute-start | bytes 24584 | tf_op jit(solution)/shard_map/ppermute | solution.py:417
  96.5 6.5 %collective-permute-start.18 = (bf16[32,2048]{1,0:T(8,128)(2,1)S(1)}, bf16[32,2048]{1,0:T(8,128)(2,1)S(1)}, u32[]{:S(2)}, u32[]{:S(2)}) collective-permute-start(bf16[32,2048]{1,0:T(8,128)(2,1)S(1)} %self_output.1), channel_id=1, source_target_pairs={{0,1},{1,0},{2,3},{3,2},{4,5},{5,4},{6,7},{7,6},{8,9},{9,8},{10,11... | collective-permute-start | bytes 393224 | tf_op jit(solution)/shard_map/ppermute | solution.py:400
  103.1 6.3 %collective-permute-start.19 = (bf16[32,2048]{1,0:T(8,128)(2,1)S(1)}, bf16[32,2048]{1,0:T(8,128)(2,1)S(1)}, u32[]{:S(2)}, u32[]{:S(2)}) collective-permute-start(bf16[32,2048]{1,0:T(8,128)(2,1)S(1)} %add_convert_fusion.1), channel_id=1, source_target_pairs={{0,2},{2,0},{1,3},{3,1},{4,6},{6,4},{5,7},{7,5},{8,10},{10,8},{9,1... | collective-permute-start | bytes 393224 | tf_op jit(solution)/shard_map/ppermute | solution.py:400

commit v3 on v2

--- a/solution.py
+++ b/solution.py
@@ -90,10 +90,10 @@
 
 def context_kernel(first, step, context_ref, w_ref, after_ref, out_ref):
     def rows_from(i, _):
-        there = pl.ds(pl.multiple_of(first + i * step, step), step)
+        there = pl.ds(pl.multiple_of(first + i * step, 128), step)
         tile = context_ref[there, :]
         product = dot(tile, w_ref[...]) * inv_rms(tile.astype(F32))
-        out_ref[pl.ds(pl.multiple_of(i * step, step), step), :] = product.astype(BF16)
+        out_ref[pl.ds(pl.multiple_of(i * step, 128), step), :] = product.astype(BF16)
         return 0
 
     lax.fori_loop(0, out_ref.shape[0] // step, rows_from, 0, unroll=True)
@@ -103,7 +103,7 @@
     width = context.shape[1]
     cols = weight.shape[1]
     return pl.pallas_call(
-        functools.partial(context_kernel, first, 512 if rows % 512 == 0 else 256),
+        functools.partial(context_kernel, first, 512 if rows % 512 == 0 else rows // 2),
         out_shape=shape_of((rows, cols)),
         in_specs=[VMEM, VMEM, pl.BlockSpec(memory_space=pl.ANY)],
         out_specs=VMEM,
@@ -131,7 +131,7 @@
 def first_project(context, weight, after, rows):
     width = context.shape[1]
     cols = weight.shape[1]
-    pieces = 4
+    pieces = 3
     return pl.pallas_call(
         first_kernel,
         out_shape=shape_of((rows, cols)),
@@ -465,7 +465,7 @@
         y_lo == 0, jnp.concatenate([own, other]), jnp.concatenate([other, own])
     )
     whole = context.shape[0]
-    part = whole // 2
+    part = whole // 8 * 3
     keys = [first_project(context, wk_cross, pair, part)]
     came = {offset: turned(pair, "b", offset) for offset in (2, 1, 3)}
     ring = [pair] + [came[offset] for offset in (1, 2, 3)]

time: 110 us -> 111 us (level)
  transfers between devices with their start and end apart: 20 -> 20, of which waited for: 12 -> 13; matrix products, arithmetic and copies ran while one was open for 0% -> 0% of each run, Pallas kernels for 23% -> 23%
where the time goes in v3:
time: 111 us; the launch traced here: 110 us
  starting transfers between devices  35.5 us (32%)
  Pallas kernels  33 us (30%)
  blocking collectives  21.4 us (19%)
  waiting for transfers between devices  18.8 us (17%)
    all_to_all x2, blocking collectives, exchanged(): return lax.all_to_all(tensor, WHOLE, 0, 0, axis_index_groups=groups)  21.4 us
    ppermute x5, starting transfers between devices, moved(): lax.ppermute(tensor, axis, [(i, (i + offset) % size) for i in range(size)])  18.9 us
    ppermute x15, starting transfers between devices, turned(): return lax.ppermute(tensor, PLANE, pairs)  16.6 us
    pallas_call x3, Pallas kernels, cross_attend(): pl.pallas_call(functools.partial(cross_kernel, offsets), out_shape=[shape...  14.5 us
    ppermute x5, waiting for transfers between devices, moved(): lax.ppermute(tensor, axis, [(i, (i + offset) % size) for i in range(size)])  9.95 us
    ppermute x15, waiting for transfers between devices, turned(): return lax.ppermute(tensor, PLANE, pairs)  8.89 us
    pallas_call x2, Pallas kernels, project_context(): pl.pallas_call(functools.partial(context_kernel, first, 512 if rows % 512...  7.42 us
    pallas_call x1, Pallas kernels, first_project(): pl.pallas_call(first_kernel, out_shape=shape_of((rows, cols)), in_specs=[...  3.49 us
  transfers between devices with their start and end apart: 20, of which 13 were waited for; matrix products, arithmetic and copies ran while one was open for 0% of the time, Pallas kernels for 23%

profile of v3, /device:TPU:1, one launch (start us, length us, event | category | flops | bytes accessed | tf_op | source)
XLA Modules:
  0.0 110.4 jit_solution(16469854450182067139)
XLA Ops:
  0.0 2.0 %queries.1 = bf16[32,512]{1,0:T(8,128)(2,1)S(1)} custom-call(bf16[32,2048]{1,0:T(8,128)(2,1)} %latent_ref.3, bf16[2048,512]{1,0:T(8,128)(2,1)} %wq_ref.2), custom_call_target="tpu_custom_call" | custom-call | flops 67108864 | bytes 2097152 | tf_op jit(solution)/shard_map/queries/pallas_call | solution.py:72
  2.0 2.2 %collective-permute-start = (bf16[32,512]{1,0:T(8,128)(2,1)S(1)}, bf16[32,512]{1,0:T(8,128)(2,1)S(1)}, u32[]{:S(2)}, u32[]{:S(2)}) collective-permute-start(bf16[32,512]{1,0:T(8,128)(2,1)S(1)} %queries.1), channel_id=1, source_target_pairs={{0,4},{4,0},{1,5},{5,1},{2,6},{6,2},{3,7},{7,3},{8,12},{12,8},{9,1... | collective-permute-start | bytes 98312 | tf_op jit(solution)/shard_map/ppermute | solution.py:400
  4.4 0.1 stack.55.ids_ref
  4.4 1.0 collective-permute-done
  5.5 2.7 %collective-permute-start.3 = (bf16[64,512]{1,0:T(8,128)(2,1)S(1)}, bf16[64,512]{1,0:T(8,128)(2,1)S(1)}, u32[]{:S(2)}, u32[]{:S(2)}) collective-permute-start(bf16[64,512]{1,0:T(8,128)(2,1)S(1)} %maximum_select_fusion.after_ref), channel_id=1, source_target_pairs={{0,24},{1,97},{8,0},{9,105},{16,8},{17,113},{24,16},{25,121},{32,5... | collective-permute-start | bytes 196616 | tf_op jit(solution)/shard_map/ppermute | solution.py:417
  8.2 0.5 collective-permute-start.2
  8.8 0.6 collective-permute-start.1
  9.4 3.5 %first_keys.1.k_ref = bf16[768,512]{1,0:T(8,128)(2,1)S(1)} custom-call(bf16[2048,2048]{1,0:T(8,128)(2,1)} %context_ref.5, bf16[2048,512]{1,0:T(8,128)(2,1)S(1)} %copy-done.1, bf16[64,512]{1,0:T(8,128)(2,1)S(1)} %maximum_select_fusion.after_ref), custom_call_target="tpu_custom_call" | custom-call | flops 1610612736 | bytes 5242880 | tf_op jit(solution)/shard_map/first_keys/pallas_call | solution.py:135
  12.9 0.6 collective-permute-done.1
  13.7 3.7 %collective-permute-start.4 = (bf16[256,512]{1,0:T(8,128)(2,1)S(1)}, bf16[256,512]{1,0:T(8,128)(2,1)S(1)}, u32[]{:S(2)}, u32[]{:S(2)}) collective-permute-start(bf16[256,512]{1,0:T(8,128)(2,1)S(1)} %pad_maximum_fusion.1.after_ref.rest_0_), channel_id=1, source_target_pairs={{0,64},{1,17},{8,72},{9,25},{16,80},{17,1},{24,88},{25,9},{32,96},... | collective-permute-start | bytes 786440 | tf_op jit(solution)/shard_map/ppermute | solution.py:417
  17.4 0.4 collective-permute-start.5
  17.8 1.0 collective-permute-start.8
  18.8 4.5 %values.1.v_ref = bf16[2048,512]{1,0:T(8,128)(2,1)S(1)} custom-call(bf16[2048,2048]{1,0:T(8,128)(2,1)S(1)} %copy-done, bf16[2048,512]{1,0:T(8,128)(2,1)S(1)} %copy-done.8, bf16[256,512]{1,0:T(8,128)(2,1)S(1)} %pad_maximum_fusion.1.after_ref.rest_0_), custom_call_target="tpu_custom_call" | custom-call | flops 4294967296 | bytes 10485760 | tf_op jit(solution)/shard_map/values/pallas_call | solution.py:105
  23.3 2.9 %keys.1.more_ref = bf16[1280,512]{1,0:T(8,128)(2,1)S(1)} custom-call(bf16[2048,2048]{1,0:T(8,128)(2,1)S(1)} %copy-done, bf16[2048,512]{1,0:T(8,128)(2,1)S(1)} %copy-done.1, bf16[256,512]{1,0:T(8,128)(2,1)S(1)} %pad_maximum_fusion.1.after_ref.rest_0_), custom_call_target="tpu_custom_call" | custom-call | flops 2684354560 | bytes 7340032 | tf_op jit(solution)/shard_map/keys/pallas_call | solution.py:105
  26.3 0.2 broadcast_in_dim.4.cut_ref
  26.5 6.8 %cross.3 = (bf16[256,640]{1,0:T(8,128)(2,1)S(1)}, bf16[256,640]{1,0:T(8,128)(2,1)S(1)}) custom-call(s32[6]{0:T(128)S(1)} %stack.55.ids_ref, s32[1024]{0:T(1024)S(1)} %broadcast_select_fusion.cutoff_ref, s32[1024,128]{1,0:T(8,128)S(1)} %broadcast_in_dim.4.cut_ref, bf16[768,512]{1,0:T(8,128)(2,1)S(1)} %first_keys.1.k_ref, bf16[1280,512]{1,0:T(8,128)(2,1)S(1)} %keys.1.more_ref, ...), custom_call_target="tpu_custom_call" | custom-call | flops 4294967296 | bytes 4194304 | tf_op jit(solution)/shard_map/cross/pallas_call | solution.py:243
  33.3 1.1 %collective-permute-start.6 = (bf16[256,640]{1,0:T(8,128)(2,1)S(1)}, bf16[256,640]{1,0:T(8,128)(2,1)S(1)}, u32[]{:S(2)}, u32[]{:S(2)}) collective-permute-start(bf16[256,640]{1,0:T(8,128)(2,1)S(1)} %get-tuple-element.16), channel_id=1, source_target_pairs={{0,64},{1,17},{8,72},{9,25},{16,80},{17,1},{24,88},{25,9},{32,96},... | collective-permute-start | bytes 983048 | tf_op jit(solution)/shard_map/ppermute | solution.py:417
  34.4 1.2 %collective-permute-start.7 = (bf16[256,640]{1,0:T(8,128)(2,1)S(1)}, bf16[256,640]{1,0:T(8,128)(2,1)S(1)}, u32[]{:S(2)}, u32[]{:S(2)}) collective-permute-start(bf16[256,640]{1,0:T(8,128)(2,1)S(1)} %get-tuple-element.17), channel_id=1, source_target_pairs={{0,32},{1,9},{8,40},{9,17},{16,48},{17,25},{24,56},{25,1},{32,64},... | collective-permute-start | bytes 983048 | tf_op jit(solution)/shard_map/ppermute | solution.py:417
  35.6 3.7 %cross.4 = bf16[256,640]{1,0:T(8,128)(2,1)S(1)} custom-call(s32[6]{0:T(128)S(1)} %stack.55.ids_ref, s32[1024]{0:T(1024)S(1)} %broadcast_select_fusion.cutoff_ref, s32[1024,128]{1,0:T(8,128)S(1)} %broadcast_in_dim.4.cut_ref, bf16[768,512]{1,0:T(8,128)(2,1)S(1)} %first_keys.1.k_ref, bf16[1280,512]{1,0:T(8,128)(2,1)S(1)} %keys.1.more_ref, ...), custom_call_target="tpu_custom_call" | custom-call | flops 2147483648 | bytes 4194304 | tf_op jit(solution)/shard_map/cross/pallas_call | solution.py:243
  39.3 1.6 %collective-permute-start.9 = (bf16[256,640]{1,0:T(8,128)(2,1)S(1)}, bf16[256,640]{1,0:T(8,128)(2,1)S(1)}, u32[]{:S(2)}, u32[]{:S(2)}) collective-permute-start(bf16[256,640]{1,0:T(8,128)(2,1)S(1)} %cross.4), channel_id=1, source_target_pairs={{0,96},{1,25},{8,104},{9,1},{16,112},{17,9},{24,120},{25,17},{32,0... | collective-permute-start | bytes 983048 | tf_op jit(solution)/shard_map/ppermute | solution.py:417
  40.9 4.0 %cross.5.d_ref = bf16[256,640]{1,0:T(8,128)(2,1)S(1)} custom-call(s32[6]{0:T(128)S(1)} %stack.55.ids_ref, s32[1024]{0:T(1024)S(1)} %broadcast_select_fusion.cutoff_ref, s32[1024,128]{1,0:T(8,128)S(1)} %broadcast_in_dim.4.cut_ref, bf16[768,512]{1,0:T(8,128)(2,1)S(1)} %first_keys.1.k_ref, bf16[1280,512]{1,0:T(8,128)(2,1)S(1)} %keys.1.more_ref, ...), custom_call_target="tpu_custom_call" | custom-call | flops 2147483648 | bytes 4194304 | tf_op jit(solution)/shard_map/cross/pallas_call | solution.py:243
  44.9 0.7 collective-permute-done.9.c_ref
  45.6 1.0 blend.1
  46.6 10.2 %all_to_all.10.parts_ref = bf16[8,32,640]{2,1,0:T(8,128)(2,1)S(1)} all-to-all(bf16[8,32,640]{2,1,0:T(8,128)(2,1)S(1)} %bitcast.21), channel_id=1, replica_groups={{0,4,8,12,16,20,24,28},{1,5,33,37,65,69,97,101},{32,36,40,44,48,52,56,6..., dimensions={0} | all-to-all | bytes 655360 | tf_op jit(solution)/shard_map/all_to_all | solution.py:427
  56.7 0.7 cross_output.1
  57.5 5.6 %collective-permute-start.10 = (bf16[32,2048]{1,0:T(8,128)(2,1)S(1)}, bf16[32,2048]{1,0:T(8,128)(2,1)S(1)}, u32[]{:S(2)}, u32[]{:S(2)}) collective-permute-start(bf16[32,2048]{1,0:T(8,128)(2,1)S(1)} %cross_output.1), channel_id=1, source_target_pairs={{0,1},{1,0},{2,3},{3,2},{4,5},{5,4},{6,7},{7,6},{8,9},{9,8},{10,11... | collective-permute-start | bytes 393224 | tf_op jit(solution)/shard_map/ppermute | solution.py:400
  63.1 1.0 collective-permute-done.10
  64.1 2.7 %collective-permute-start.11 = (bf16[32,2048]{1,0:T(8,128)(2,1)S(1)}, bf16[32,2048]{1,0:T(8,128)(2,1)S(1)}, u32[]{:S(2)}, u32[]{:S(2)}) collective-permute-start(bf16[32,2048]{1,0:T(8,128)(2,1)S(1)} %add_convert_fusion.2.one_ref), channel_id=1, source_target_pairs={{0,2},{2,0},{1,3},{3,1},{4,6},{6,4},{5,7},{7,5},{8,10},{10,8},{9,1... | collective-permute-start | bytes 393224 | tf_op jit(solution)/shard_map/ppermute | solution.py:400
  66.8 3.6 %collective-permute-done.11.two_ref = bf16[32,2048]{1,0:T(8,128)(2,1)S(1)} collective-permute-done((bf16[32,2048]{1,0:T(8,128)(2,1)S(1)}, bf16[32,2048]{1,0:T(8,128)(2,1)S(1)}, u32[]{:S(2)}, u32[]{:S(2)}) %collective-permute-start.11) | collective-permute-done | bytes 131104 | tf_op jit(solution)/shard_map/ppermute | solution.py:400
  70.4 1.8 %self_project.1 = (f32[32,2048]{1,0:T(8,128)S(1)}, bf16[32,384]{1,0:T(8,128)(2,1)S(1)}, bf16[32,384]{1,0:T(8,128)(2,1)S(1)}, bf16[32,384]{1,0:T(8,128)(2,1)S(1)}, bf16[32,384]{1,0:T(8,128)(2,1)S(1)}) custom-call(s32[6]{0:T(128)S(1)} %stack.55.ids_ref, bf16[32,2048]{1,0:T(8,128)(2,1)S(1)} %copy-done.7, bf16[32,2048]{1,0:T(8,128)(2,1)S(1)} %add_convert_fusion.2.one_ref, ...), custom_call_target="tpu_custom_call" | custom-call | tf_op jit(solution)/shard_map/self_project/pallas_call | solution.py:331
  72.3 1.0 collective-permute-start.14
  73.2 1.2 %collective-permute-start.13 = (bf16[32,384]{1,0:T(8,128)(2,1)S(1)}, bf16[32,384]{1,0:T(8,128)(2,1)S(1)}, u32[]{:S(2)}, u32[]{:S(2)}) collective-permute-start(bf16[32,384]{1,0:T(8,128)(2,1)S(1)} %get-tuple-element.21), channel_id=1, source_target_pairs={{0,64},{1,17},{8,72},{9,25},{16,80},{17,1},{24,88},{25,9},{32,96},... | collective-permute-start | bytes 73736 | tf_op jit(solution)/shard_map/ppermute | solution.py:417
  74.4 0.6 collective-permute-done.14.d_ref
  75.0 2.4 %collective-permute-done.13.c_ref = bf16[32,384]{1,0:T(8,128)(2,1)S(1)} collective-permute-done((bf16[32,384]{1,0:T(8,128)(2,1)S(1)}, bf16[32,384]{1,0:T(8,128)(2,1)S(1)}, u32[]{:S(2)}, u32[]{:S(2)}) %collective-permute-start.13) | collective-permute-done | bytes 24608 | tf_op jit(solution)/shard_map/ppermute | solution.py:417
  77.4 0.9 collective-permute-done.12.b_ref
  78.3 11.2 %all_to_all.11.kv_ref = bf16[8,128,256]{2,1,0:T(8,128)(2,1)S(1)} all-to-all(bf16[8,128,256]{2,1,0:T(8,128)(2,1)S(1)} %broadcast_in_dim.5), channel_id=1, replica_groups={{0,4,8,12,16,20,24,28},{1,5,33,37,65,69,97,101},{32,36,40,44,48,52,56,6..., dimensions={0} | all-to-all | bytes 1048576 | tf_op jit(solution)/shard_map/all_to_all | solution.py:427
  89.5 1.1 %self_attend.1 = (bf16[32,128]{1,0:T(8,128)(2,1)S(1)}, bf16[32,128]{1,0:T(8,128)(2,1)S(1)}, bf16[32,128]{1,0:T(8,128)(2,1)S(1)}, bf16[32,128]{1,0:T(8,128)(2,1)S(1)}) custom-call(s32[6]{0:T(128)S(1)} %stack.55.ids_ref, bf16[32,384]{1,0:T(8,128)(2,1)S(1)} %get-tuple-element.19.a_ref, bf16[32,384]{1,0:T(8,128)(2,1)S(1)} %collective-permute-done.12.b_ref, ...), custom_call_target="tpu_custom_call" | custom-call | tf_op jit(solution)/shard_map/self_attend/pallas_call | solution.py:369
  90.7 0.8 collective-permute-start.15
  91.5 0.7 collective-permute-start.16
  92.2 1.0 collective-permute-done.15.b_ref
  93.3 2.2 %collective-permute-done.16.c_ref = bf16[32,128]{1,0:T(8,128)(2,1)S(1)} collective-permute-done((bf16[32,128]{1,0:T(8,128)(2,1)S(1)}, bf16[32,128]{1,0:T(8,128)(2,1)S(1)}, u32[]{:S(2)}, u32[]{:S(2)}) %collective-permute-start.16) | collective-permute-done | bytes 8224 | tf_op jit(solution)/shard_map/ppermute | solution.py:417
  95.5 0.4 collective-permute-done.17.d_ref
  95.9 1.0 self_output.1
  96.9 5.5 %collective-permute-start.18 = (bf16[32,2048]{1,0:T(8,128)(2,1)S(1)}, bf16[32,2048]{1,0:T(8,128)(2,1)S(1)}, u32[]{:S(2)}, u32[]{:S(2)}) collective-permute-start(bf16[32,2048]{1,0:T(8,128)(2,1)S(1)} %self_output.1), channel_id=1, source_target_pairs={{0,1},{1,0},{2,3},{3,2},{4,5},{5,4},{6,7},{7,6},{8,9},{9,8},{10,11... | collective-permute-start | bytes 393224 | tf_op jit(solution)/shard_map/ppermute | solution.py:400
  102.4 1.0 collective-permute-done.18
  103.4 3.0 %collective-permute-start.19 = (bf16[32,2048]{1,0:T(8,128)(2,1)S(1)}, bf16[32,2048]{1,0:T(8,128)(2,1)S(1)}, u32[]{:S(2)}, u32[]{:S(2)}) collective-permute-start(bf16[32,2048]{1,0:T(8,128)(2,1)S(1)} %add_convert_fusion.1), channel_id=1, source_target_pairs={{0,2},{2,0},{1,3},{3,1},{4,6},{6,4},{5,7},{7,5},{8,10},{10,8},{9,1... | collective-permute-start | bytes 393224 | tf_op jit(solution)/shard_map/ppermute | solution.py:400
  106.4 3.3 %collective-permute-done.19 = bf16[32,2048]{1,0:T(8,128)(2,1)S(1)} collective-permute-done((bf16[32,2048]{1,0:T(8,128)(2,1)S(1)}, bf16[32,2048]{1,0:T(8,128)(2,1)S(1)}, u32[]{:S(2)}, u32[]{:S(2)}) %collective-permute-start.19) | collective-permute-done | bytes 131104 | tf_op jit(solution)/shard_map/ppermute | solution.py:400
  109.7 0.7 add_convert_fusion
  (46 shorter events, 0.5 us)
Async XLA Ops:
  0.0 4.2 %copy-start.9 = (s32[1024]{0:T(1024)S(1)}, s32[1024]{0:T(1024)}, u32[]{:S(2)}) copy-start(s32[1024]{0:T(1024)} %param.13) | copy-start | bytes 12292
  0.0 9.4 %copy-start.1 = (bf16[2048,512]{1,0:T(8,128)(2,1)S(1)}, bf16[2048,512]{1,0:T(8,128)(2,1)}, u32[]{:S(2)}) copy-start(bf16[2048,512]{1,0:T(8,128)(2,1)} %w_ref.4) | copy-start | bytes 6291460
  2.0 3.5 %collective-permute-start = (bf16[32,512]{1,0:T(8,128)(2,1)S(1)}, bf16[32,512]{1,0:T(8,128)(2,1)S(1)}, u32[]{:S(2)}, u32[]{:S(2)}) collective-permute-start(bf16[32,512]{1,0:T(8,128)(2,1)S(1)} %queries.1), channel_id=1, source_target_pairs={{0,4},{4,0},{1,5},{5,1},{2,6},{6,2},{3,7},{7,3},{8,12},{12,8},{9,1... | collective-permute-start | bytes 98312 | tf_op jit(solution)/shard_map/ppermute | solution.py:400
  5.5 13.3 %copy-start = (bf16[2048,2048]{1,0:T(8,128)(2,1)S(1)}, bf16[2048,2048]{1,0:T(8,128)(2,1)}, u32[]{:S(2)}) copy-start(bf16[2048,2048]{1,0:T(8,128)(2,1)} %context_ref.5) | copy-start | bytes 25165828
  5.5 13.3 %copy-start.8 = (bf16[2048,512]{1,0:T(8,128)(2,1)S(1)}, bf16[2048,512]{1,0:T(8,128)(2,1)}, u32[]{:S(2)}) copy-start(bf16[2048,512]{1,0:T(8,128)(2,1)} %w_ref.5) | copy-start | bytes 6291460
  5.5 7.4 %collective-permute-start.3 = (bf16[64,512]{1,0:T(8,128)(2,1)S(1)}, bf16[64,512]{1,0:T(8,128)(2,1)S(1)}, u32[]{:S(2)}, u32[]{:S(2)}) collective-permute-start(bf16[64,512]{1,0:T(8,128)(2,1)S(1)} %maximum_select_fusion.after_ref), channel_id=1, source_target_pairs={{0,24},{1,97},{8,0},{9,105},{16,8},{17,113},{24,16},{25,121},{32,5... | collective-permute-start | bytes 196616 | tf_op jit(solution)/shard_map/ppermute | solution.py:417
  8.2 4.7 %collective-permute-start.2 = (bf16[64,512]{1,0:T(8,128)(2,1)S(1)}, bf16[64,512]{1,0:T(8,128)(2,1)S(1)}, u32[]{:S(2)}, u32[]{:S(2)}) collective-permute-start(bf16[64,512]{1,0:T(8,128)(2,1)S(1)} %maximum_select_fusion.after_ref), channel_id=1, source_target_pairs={{0,16},{1,65},{8,24},{9,73},{16,0},{17,81},{24,8},{25,89},{32,48},... | collective-permute-start | bytes 196616 | tf_op jit(solution)/shard_map/ppermute | solution.py:417
  8.8 4.8 %collective-permute-start.1 = (bf16[64,512]{1,0:T(8,128)(2,1)S(1)}, bf16[64,512]{1,0:T(8,128)(2,1)S(1)}, u32[]{:S(2)}, u32[]{:S(2)}) collective-permute-start(bf16[64,512]{1,0:T(8,128)(2,1)S(1)} %maximum_select_fusion.after_ref), channel_id=1, source_target_pairs={{0,8},{1,33},{8,16},{9,41},{16,24},{17,49},{24,0},{25,57},{32,40},... | collective-permute-start | bytes 196616 | tf_op jit(solution)/shard_map/ppermute | solution.py:417
  13.7 12.6 %collective-permute-start.4 = (bf16[256,512]{1,0:T(8,128)(2,1)S(1)}, bf16[256,512]{1,0:T(8,128)(2,1)S(1)}, u32[]{:S(2)}, u32[]{:S(2)}) collective-permute-start(bf16[256,512]{1,0:T(8,128)(2,1)S(1)} %pad_maximum_fusion.1.after_ref.rest_0_), channel_id=1, source_target_pairs={{0,64},{1,17},{8,72},{9,25},{16,80},{17,1},{24,88},{25,9},{32,96},... | collective-permute-start | bytes 786440 | tf_op jit(solution)/shard_map/ppermute | solution.py:417
  17.4 8.9 %collective-permute-start.5 = (bf16[256,512]{1,0:T(8,128)(2,1)S(1)}, bf16[256,512]{1,0:T(8,128)(2,1)S(1)}, u32[]{:S(2)}, u32[]{:S(2)}) collective-permute-start(bf16[256,512]{1,0:T(8,128)(2,1)S(1)} %pad_maximum_fusion.1.after_ref.rest_0_), channel_id=1, source_target_pairs={{0,96},{1,25},{8,104},{9,1},{16,112},{17,9},{24,120},{25,17},{32,0... | collective-permute-start | bytes 786440 | tf_op jit(solution)/shard_map/ppermute | solution.py:417
  17.8 17.8 %collective-permute-start.8 = (bf16[256,512]{1,0:T(8,128)(2,1)S(1)}, bf16[256,512]{1,0:T(8,128)(2,1)S(1)}, u32[]{:S(2)}, u32[]{:S(2)}) collective-permute-start(bf16[256,512]{1,0:T(8,128)(2,1)S(1)} %pad_maximum_fusion.1.after_ref.rest_0_), channel_id=1, source_target_pairs={{0,32},{1,9},{8,40},{9,17},{16,48},{17,25},{24,56},{25,1},{32,64},... | collective-permute-start | bytes 786440 | tf_op jit(solution)/shard_map/ppermute | solution.py:417
  33.3 11.6 %collective-permute-start.6 = (bf16[256,640]{1,0:T(8,128)(2,1)S(1)}, bf16[256,640]{1,0:T(8,128)(2,1)S(1)}, u32[]{:S(2)}, u32[]{:S(2)}) collective-permute-start(bf16[256,640]{1,0:T(8,128)(2,1)S(1)} %get-tuple-element.16), channel_id=1, source_target_pairs={{0,64},{1,17},{8,72},{9,25},{16,80},{17,1},{24,88},{25,9},{32,96},... | collective-permute-start | bytes 983048 | tf_op jit(solution)/shard_map/ppermute | solution.py:417
  34.4 10.5 %collective-permute-start.7 = (bf16[256,640]{1,0:T(8,128)(2,1)S(1)}, bf16[256,640]{1,0:T(8,128)(2,1)S(1)}, u32[]{:S(2)}, u32[]{:S(2)}) collective-permute-start(bf16[256,640]{1,0:T(8,128)(2,1)S(1)} %get-tuple-element.17), channel_id=1, source_target_pairs={{0,32},{1,9},{8,40},{9,17},{16,48},{17,25},{24,56},{25,1},{32,64},... | collective-permute-start | bytes 983048 | tf_op jit(solution)/shard_map/ppermute | solution.py:417
  39.3 6.3 %collective-permute-start.9 = (bf16[256,640]{1,0:T(8,128)(2,1)S(1)}, bf16[256,640]{1,0:T(8,128)(2,1)S(1)}, u32[]{:S(2)}, u32[]{:S(2)}) collective-permute-start(bf16[256,640]{1,0:T(8,128)(2,1)S(1)} %cross.4), channel_id=1, source_target_pairs={{0,96},{1,25},{8,104},{9,1},{16,112},{17,9},{24,120},{25,17},{32,0... | collective-permute-start | bytes 983048 | tf_op jit(solution)/shard_map/ppermute | solution.py:417
  40.9 29.5 %copy-start.5 = (bf16[2048,512]{1,0:T(8,128)(2,1)S(1)}, bf16[2048,512]{1,0:T(8,128)(2,1)}, u32[]{:S(2)}) copy-start(bf16[2048,512]{1,0:T(8,128)(2,1)} %wk_ref.1) | copy-start | bytes 6291460
  40.9 29.5 %copy-start.6 = (bf16[2048,512]{1,0:T(8,128)(2,1)S(1)}, bf16[2048,512]{1,0:T(8,128)(2,1)}, u32[]{:S(2)}) copy-start(bf16[2048,512]{1,0:T(8,128)(2,1)} %wv_ref.1) | copy-start | bytes 6291460
  44.9 11.9 %copy-start.2 = (bf16[512,2048]{1,0:T(8,128)(2,1)S(1)}, bf16[512,2048]{1,0:T(8,128)(2,1)}, u32[]{:S(2)}) copy-start(bf16[512,2048]{1,0:T(8,128)(2,1)} %wo_ref.2) | copy-start | bytes 6291460
  46.6 23.8 %copy-start.4 = (bf16[2048,512]{1,0:T(8,128)(2,1)S(1)}, bf16[2048,512]{1,0:T(8,128)(2,1)}, u32[]{:S(2)}) copy-start(bf16[2048,512]{1,0:T(8,128)(2,1)} %wq_ref.3) | copy-start | bytes 6291460
  46.6 23.8 %copy-start.7 = (bf16[32,2048]{1,0:T(8,128)(2,1)S(1)}, bf16[32,2048]{1,0:T(8,128)(2,1)}, u32[]{:S(2)}) copy-start(bf16[32,2048]{1,0:T(8,128)(2,1)} %latent_ref.3) | copy-start | bytes 393220
  57.5 6.5 %collective-permute-start.10 = (bf16[32,2048]{1,0:T(8,128)(2,1)S(1)}, bf16[32,2048]{1,0:T(8,128)(2,1)S(1)}, u32[]{:S(2)}, u32[]{:S(2)}) collective-permute-start(bf16[32,2048]{1,0:T(8,128)(2,1)S(1)} %cross_output.1), channel_id=1, source_target_pairs={{0,1},{1,0},{2,3},{3,2},{4,5},{5,4},{6,7},{7,6},{8,9},{9,8},{10,11... | collective-permute-start | bytes 393224 | tf_op jit(solution)/shard_map/ppermute | solution.py:400
  64.1 6.3 %collective-permute-start.11 = (bf16[32,2048]{1,0:T(8,128)(2,1)S(1)}, bf16[32,2048]{1,0:T(8,128)(2,1)S(1)}, u32[]{:S(2)}, u32[]{:S(2)}) collective-permute-start(bf16[32,2048]{1,0:T(8,128)(2,1)S(1)} %add_convert_fusion.2.one_ref), channel_id=1, source_target_pairs={{0,2},{2,0},{1,3},{3,1},{4,6},{6,4},{5,7},{7,5},{8,10},{10,8},{9,1... | collective-permute-start | bytes 393224 | tf_op jit(solution)/shard_map/ppermute | solution.py:400
  72.2 23.7 %copy-start.3 = (bf16[512,2048]{1,0:T(8,128)(2,1)S(1)}, bf16[512,2048]{1,0:T(8,128)(2,1)}, u32[]{:S(2)}) copy-start(bf16[512,2048]{1,0:T(8,128)(2,1)} %wo_ref.3) | copy-start | bytes 6291460
  72.3 2.7 %collective-permute-start.14 = (bf16[32,384]{1,0:T(8,128)(2,1)S(1)}, bf16[32,384]{1,0:T(8,128)(2,1)S(1)}, u32[]{:S(2)}, u32[]{:S(2)}) collective-permute-start(bf16[32,384]{1,0:T(8,128)(2,1)S(1)} %get-tuple-element.22), channel_id=1, source_target_pairs={{0,96},{1,25},{8,104},{9,1},{16,112},{17,9},{24,120},{25,17},{32,0... | collective-permute-start | bytes 73736 | tf_op jit(solution)/shard_map/ppermute | solution.py:417
  73.2 4.2 %collective-permute-start.13 = (bf16[32,384]{1,0:T(8,128)(2,1)S(1)}, bf16[32,384]{1,0:T(8,128)(2,1)S(1)}, u32[]{:S(2)}, u32[]{:S(2)}) collective-permute-start(bf16[32,384]{1,0:T(8,128)(2,1)S(1)} %get-tuple-element.21), channel_id=1, source_target_pairs={{0,64},{1,17},{8,72},{9,25},{16,80},{17,1},{24,88},{25,9},{32,96},... | collective-permute-start | bytes 73736 | tf_op jit(solution)/shard_map/ppermute | solution.py:417
  74.4 3.9 %collective-permute-start.12 = (bf16[32,384]{1,0:T(8,128)(2,1)S(1)}, bf16[32,384]{1,0:T(8,128)(2,1)S(1)}, u32[]{:S(2)}, u32[]{:S(2)}) collective-permute-start(bf16[32,384]{1,0:T(8,128)(2,1)S(1)} %get-tuple-element.20), channel_id=1, source_target_pairs={{0,32},{1,9},{8,40},{9,17},{16,48},{17,25},{24,56},{25,1},{32,64},... | collective-permute-start | bytes 73736 | tf_op jit(solution)/shard_map/ppermute | solution.py:417
  90.7 2.6 %collective-permute-start.15 = (bf16[32,128]{1,0:T(8,128)(2,1)S(1)}, bf16[32,128]{1,0:T(8,128)(2,1)S(1)}, u32[]{:S(2)}, u32[]{:S(2)}) collective-permute-start(bf16[32,128]{1,0:T(8,128)(2,1)S(1)} %get-tuple-element.24), channel_id=1, source_target_pairs={{0,96},{1,25},{8,104},{9,1},{16,112},{17,9},{24,120},{25,17},{32,0... | collective-permute-start | bytes 24584 | tf_op jit(solution)/shard_map/ppermute | solution.py:417
  91.5 4.0 %collective-permute-start.16 = (bf16[32,128]{1,0:T(8,128)(2,1)S(1)}, bf16[32,128]{1,0:T(8,128)(2,1)S(1)}, u32[]{:S(2)}, u32[]{:S(2)}) collective-permute-start(bf16[32,128]{1,0:T(8,128)(2,1)S(1)} %get-tuple-element.25), channel_id=1, source_target_pairs={{0,64},{1,17},{8,72},{9,25},{16,80},{17,1},{24,88},{25,9},{32,96},... | collective-permute-start | bytes 24584 | tf_op jit(solution)/shard_map/ppermute | solution.py:417
  92.2 3.7 %collective-permute-start.17 = (bf16[32,128]{1,0:T(8,128)(2,1)S(1)}, bf16[32,128]{1,0:T(8,128)(2,1)S(1)}, u32[]{:S(2)}, u32[]{:S(2)}) collective-permute-start(bf16[32,128]{1,0:T(8,128)(2,1)S(1)} %get-tuple-element.26), channel_id=1, source_target_pairs={{0,32},{1,9},{8,40},{9,17},{16,48},{17,25},{24,56},{25,1},{32,64},... | collective-permute-start | bytes 24584 | tf_op jit(solution)/shard_map/ppermute | solution.py:417
  96.9 6.5 %collective-permute-start.18 = (bf16[32,2048]{1,0:T(8,128)(2,1)S(1)}, bf16[32,2048]{1,0:T(8,128)(2,1)S(1)}, u32[]{:S(2)}, u32[]{:S(2)}) collective-permute-start(bf16[32,2048]{1,0:T(8,128)(2,1)S(1)} %self_output.1), channel_id=1, source_target_pairs={{0,1},{1,0},{2,3},{3,2},{4,5},{5,4},{6,7},{7,6},{8,9},{9,8},{10,11... | collective-permute-start | bytes 393224 | tf_op jit(solution)/shard_map/ppermute | solution.py:400
  103.4 6.3 %collective-permute-start.19 = (bf16[32,2048]{1,0:T(8,128)(2,1)S(1)}, bf16[32,2048]{1,0:T(8,128)(2,1)S(1)}, u32[]{:S(2)}, u32[]{:S(2)}) collective-permute-start(bf16[32,2048]{1,0:T(8,128)(2,1)S(1)} %add_convert_fusion.1), channel_id=1, source_target_pairs={{0,2},{2,0},{1,3},{3,1},{4,6},{6,4},{5,7},{7,5},{8,10},{10,8},{9,1... | collective-permute-start | bytes 393224 | tf_op jit(solution)/shard_map/ppermute | solution.py:400
